TPU v7x, 32 devices: a whole 2x2x4 slice. The times are simulated.
32 devices in a mesh: groups: 2 (over x), worker: 2 (over core), tensor: 8 (over z, y).
Axes of the slice: x: 2, y: 2, z: 4, core: 2. Of those that a mesh axis runs over, the one named last changes fastest.
Arguments:
- tokens: bfloat16 [1024, 8192], P(('groups', 'worker'), 'tensor'), parts along dimension 0, may hold values from -6 to 6
- norm_gain: float32 [8192], replicated, may hold values from 0.5 to 1.5
- query_weight: bfloat16 [8192, 8192], P(None, 'tensor'), may hold values from -0.0625 to 0.0625
- key_weight: bfloat16 [8192, 1024], P(None, 'tensor'), may hold values from -0.15625 to 0.15625
- value_weight: bfloat16 [8192, 1024], P(None, 'tensor'), may hold values from -0.0625 to 0.0625
- output_weight: bfloat16 [8192, 8192], P('tensor'), may hold values from -0.0625 to 0.0625
- cached_blocks: bfloat16 [8, 1024, 2, 1024], P(('groups', 'worker'), 'tensor'), parts along dimension 0
- cache_length: int32 [8], P('groups'), parts along dimension 0, may hold values from 256 to 1024, as said below
- block_table: int32 [8, 64], P('groups'), parts along dimension 0, may hold values from 0 to 63, each once within a row
- destination: int32 [8], P('groups'), parts along dimension 0, may hold values from 0 to 1, as said below
Outputs:
- attended: bfloat16 [4, 3, 128, 8192], P(('groups', 'worker'), None, None, 'tensor'), parts along dimension 0
There are 2 independent parts, one for each index of `groups`. A program takes and returns all parts, laid end to end along the dimension named above; an argument that names none is the same for every part. Nothing has to cross between parts.
Inputs may be any that keep to these rules, and one draw needn't show every extreme that they name: Exactly 3 sequences have one destination, the others the other; which one is drawn. `cache_length`: some sequence has exactly 1024 cached tokens.
All inputs are finite; a program needn't handle non-finite values.
Results may differ from a plain program's by a relative error of at most 0.02.
The roundings to bfloat16 on the way count: a program that leaves them out, or rounds other values in their place, can miss the bound.
Values may be sent and summed in bfloat16 or wider, within the bound.
A program may use at most 128 MiB of HBM per device.

v0:
```python
import math

import jax
import jax.numpy as jnp
from jax import lax
from jax.sharding import PartitionSpec as P

D = 8192
KVH = 8
HD = 128
NEW = 128
BLK = 16
CAP = 3


epsilon = 1e-05


def from_partner(block, axis, bit):
    count = lax.axis_size(axis)
    route = []
    for low in range(count):
        high = low | 1 << bit
        if high != low and high < count:
            route += [(low, high), (high, low)]
    return lax.ppermute(block, axis, route)


def rotate(values, positions):
    halfway = HD // 2
    inverse = 500000.0 ** (-(jnp.arange(halfway, dtype=jnp.float32) * 2.0 / HD))
    angles = positions[:, None] * inverse[None, :]
    cosine_table = jnp.concatenate([jnp.cos(angles), jnp.cos(angles)], axis=-1)[:, None, :]
    sine_table = jnp.concatenate([jnp.sin(angles), jnp.sin(angles)], axis=-1)[:, None, :]
    turned = jnp.concatenate([-values[..., halfway:], values[..., :halfway]], axis=-1)
    return values * cosine_table + turned * sine_table


def attend(
    token_rows,
    blocks,
    lengths,
    tables,
    norm_gain,
    query_weight,
    key_weight,
    value_weight,
    output_weight,
):
    tensor_count = lax.axis_size("tensor")
    tensor_index = lax.axis_index("tensor")
    group_width = tensor_count // KVH
    bit_count = group_width.bit_length() - 1
    seq_count = blocks.shape[0]
    total = token_rows.shape[0]
    query_cols = query_weight.shape[1]
    widened = lax.all_gather(token_rows, "tensor", axis=1, tiled=True).astype(jnp.float32)
    scaled = (widened * norm_gain[None, :]).astype(jnp.bfloat16)
    query_sum = jnp.dot(scaled, query_weight, preferred_element_type=jnp.float32)
    key_sum = jnp.dot(scaled, key_weight, preferred_element_type=jnp.float32)
    value_sum = jnp.dot(scaled, value_weight, preferred_element_type=jnp.float32)
    squares = jnp.sum(widened * widened, axis=1)
    factor = lax.rsqrt(squares / D + epsilon)[:, None]
    positions = (
        (lengths[:, None] + jnp.arange(NEW, dtype=jnp.int32)[None, :])
        .reshape(total)
        .astype(jnp.float32)
    )
    heads_here = query_cols // HD
    queries = rotate((query_sum * factor).reshape(total, heads_here, HD), positions).astype(
        jnp.bfloat16
    )
    key_full = (key_sum * factor).astype(jnp.bfloat16)
    value_full = (value_sum * factor).astype(jnp.bfloat16)
    for bit in range(bit_count):
        other_key, other_value = from_partner((key_full, value_full), "tensor", bit)
        upper = tensor_index // (1 << bit) % 2 == 1
        key_full = jnp.where(
            upper,
            jnp.concatenate([other_key, key_full], axis=1),
            jnp.concatenate([key_full, other_key], axis=1),
        )
        value_full = jnp.where(
            upper,
            jnp.concatenate([other_value, value_full], axis=1),
            jnp.concatenate([value_full, other_value], axis=1),
        )
    new_key = rotate(key_full.astype(jnp.float32)[:, None, :], positions)[:, 0, :].astype(
        jnp.bfloat16
    )
    fresh_keys = new_key.reshape(seq_count, NEW, HD)
    fresh_values = value_full.reshape(seq_count, NEW, HD)
    local_tokens = blocks.shape[1]
    inverse_root = 1.0 / math.sqrt(HD)
    query_blocks = queries.reshape(seq_count, NEW, heads_here, HD)
    causal = jnp.arange(NEW)[:, None] >= jnp.arange(NEW)[None, :]
    spread = jnp.repeat(
        blocks.reshape(seq_count, local_tokens, 2, KVH, HD), tensor_count // KVH, axis=3
    )
    arrived = lax.all_to_all(spread, "tensor", split_axis=3, concat_axis=1, tiled=True)
    context = arrived.shape[1]
    old_key = arrived[:, :, 0, 0, :]
    old_value = arrived[:, :, 1, 0, :]
    stored = jnp.arange(context, dtype=jnp.int32)
    logical = jnp.take(tables, stored // BLK, axis=1) * BLK + stored % BLK
    visible = logical < lengths[:, None]
    old_scores = (
        jnp.einsum("sqhd,skd->shqk", query_blocks, old_key, preferred_element_type=jnp.float32)
        * inverse_root
    )
    old_scores = jnp.where(visible[:, None, None, :], old_scores, -1e30)
    new_scores = (
        jnp.einsum("sqhd,skd->shqk", query_blocks, fresh_keys, preferred_element_type=jnp.float32)
        * inverse_root
    )
    new_scores = jnp.where(causal[None, None], new_scores, -1e30)
    largest = jnp.maximum(jnp.max(old_scores, axis=3), jnp.max(new_scores, axis=3))[..., None]
    old_expo = jnp.exp(old_scores - largest)
    new_expo = jnp.exp(new_scores - largest)
    denominator = (jnp.sum(old_expo, axis=3) + jnp.sum(new_expo, axis=3))[..., None]
    old_probs = (old_expo / denominator).astype(jnp.bfloat16)
    new_probs = (new_expo / denominator).astype(jnp.bfloat16)
    mixture = jnp.einsum("shqk,skd->sqhd", old_probs, old_value, preferred_element_type=jnp.float32)
    mixture = mixture + jnp.einsum(
        "shqk,skd->sqhd", new_probs, fresh_values, preferred_element_type=jnp.float32
    )
    attended_rows = mixture.astype(jnp.bfloat16).reshape(total, heads_here * HD)
    partial_value = jnp.dot(attended_rows, output_weight, preferred_element_type=jnp.float32)
    summed = lax.psum_scatter(partial_value, "tensor", scatter_dimension=1, tiled=True)
    return summed.astype(jnp.bfloat16)


def local(
    tokens,
    norm_gain,
    query_weight,
    key_weight,
    value_weight,
    output_weight,
    cached_blocks,
    cache_length,
    block_table,
    destination,
):
    worker_index = lax.axis_index("worker")
    seq_total = destination.shape[0]
    belongs = (destination == worker_index).astype(jnp.int32)
    ranking = jnp.cumsum(belongs) - 1
    matched = (belongs[None, :] == 1) & (
        ranking[None, :] == jnp.arange(CAP, dtype=jnp.int32)[:, None]
    )
    slot_owner = jnp.sum(
        matched.astype(jnp.int32) * jnp.arange(seq_total, dtype=jnp.int32)[None, :], axis=1
    )
    occupied = jnp.any(matched, axis=1)
    local_count = cached_blocks.shape[0]
    owned = worker_index * local_count + jnp.arange(local_count, dtype=jnp.int32)
    mixed = attend(
        tokens,
        cached_blocks,
        jnp.take(cache_length, owned),
        jnp.take(block_table, owned, axis=0),
        norm_gain,
        query_weight,
        key_weight,
        value_weight,
        output_weight,
    )
    everyone = lax.all_gather(mixed, "worker", axis=0, tiled=True)
    placed = jnp.take(everyone.reshape(seq_total, NEW, -1), slot_owner, axis=0)
    result = jnp.where(occupied[:, None, None], placed, jnp.zeros_like(placed))
    return result[None]


def solution(mesh):
    placed = (
        P(("groups", "worker"), "tensor"),
        P(),
        P(None, "tensor"),
        P(None, "tensor"),
        P(None, "tensor"),
        P("tensor", None),
        P(("groups", "worker"), "tensor", None, None),
        P("groups"),
        P("groups", None),
        P("groups"),
    )
    return jax.shard_map(
        local,
        mesh=mesh,
        in_specs=placed,
        out_specs=P(("groups", "worker"), None, None, "tensor"),
        check_vma=False,
    )
```

profile of v0, /device:TPU:0, one launch (start us, length us, event | category | flops | bytes accessed | tf_op | source)
XLA Modules:
  0.0 312.3 jit_solution(4129475814052174620)
XLA Ops:
  7.3 2.6 copy.86
  9.8 1.3 copy.87
  11.1 7.3 %all-to-all-start = ((bf16[2,128,2,8,128]{4,1,0,2,3:T(8,128)(2,1)}), bf16[2,128,2,8,128]{4,1,0,2,3:T(8,128)(2,1)S(1)}, u32[]{:S(2)}, u32[]{:S(2)}) async-start(bf16[2,128,2,8,128]{4,1,0,2,3:T(8,128)(2,1)} %copy.87), calls=%async_computation | async-start | bytes 2097152 | tf_op jit(solution)/shard_map/all_to_all | solution.py:100
  18.5 1.3 gather_fusion.2
  19.8 1.2 gather_fusion
  21.3 4.0 %gather_fusion.1 = s32[1024,2]{1,0:T(8,128)} fusion(s32[2,64]{0,1:T(8,128)S(1)} %copy.80, s32[1024]{0:T(1024)S(1)} %broadcast_clamp_fusion), kind=kCustom, calls=%fused_computation.1 | custom fusion | bytes 20480 | tf_op jit(solution)/shard_map/jit(_take)/gather | solution.py:105
  25.3 1.2 copy.81
  28.3 32.7 %all-to-all-done = bf16[2,128,2,8,128]{4,1,0,2,3:T(8,128)(2,1)S(1)} async-done(((bf16[2,128,2,8,128]{4,1,0,2,3:T(8,128)(2,1)}), bf16[2,128,2,8,128]{4,1,0,2,3:T(8,128)(2,1)S(1)}, u32[]{:S(2)}, u32[]{:S(2)}) %all-to-all-start) | async-done | bytes 1048608 | tf_op jit(solution)/shard_map/all_to_all | solution.py:100
  62.1 40.9 %all-gather.3.cloned.1.call-done = bf16[256,8192]{1,0:T(8,128)(2,1)} async-done(((bf16[256,1024]{1,0:T(8,128)(2,1)}), bf16[256,8192]{1,0:T(8,128)(2,1)}) %all-gather.3.cloned.1.call-update) | async-done | bytes 4194320 | tf_op jit(solution)/shard_map/all_gather | solution.py:57
  102.9 3.1 fusion.1
  106.1 3.6 %fusion.25 = bf16[256,128]{0,1:T(8,128)(2,1)S(1)} fusion(bf16[8192,128]{1,0:T(8,128)(2,1)S(1)} %copy-done, bf16[256,8192]{1,0:T(8,128)(2,1)} %all-gather.3.cloned.1.call-done, f32[8192]{0:T(1024)} %param.11, f32[256]{0:T(256)S(1)} %add_rsqrt_fusion), kind=kOutput, calls=%fused_computation.28 | convolution fusion | flops 543227904 | bytes 6390784 | tf_op jit(solution)/shard_map/dot_general | solution.py:61
  110.3 4.3 %fusion.31 = f32[256,128]{0,1:T(8,128)S(1)} fusion(bf16[8192,128]{1,0:T(8,128)(2,1)} %param.13, bf16[256,8192]{1,0:T(8,128)(2,1)} %all-gather.3.cloned.1.call-done, f32[8192]{0:T(1024)S(1)} %copy-done.6, f32[256]{0:T(256)S(1)} %add_rsqrt_fusion), kind=kOutput, calls=%fused_computation.30 | convolution fusion | flops 543260672 | bytes 6456320 | tf_op jit(solution)/shard_map/dot_general | solution.py:60
  114.8 9.5 %fusion.11 = f32[256,1024]{1,0:T(8,128)S(1)} fusion(bf16[8192,1024]{1,0:T(8,128)(2,1)} %param.12, bf16[256,8192]{1,0:T(8,128)(2,1)} %all-gather.3.cloned.1.call-done, f32[8192]{0:T(1024)} %param.11, f32[256]{0:T(256)S(1)} %add_rsqrt_fusion), kind=kOutput, calls=%fused_computation.18 | convolution fusion | flops 4301520896 | bytes 22053888 | tf_op jit(solution)/shard_map/dot_general | solution.py:59
  126.2 1.5 copy.105
  128.4 2.6 bitcast_reduce_fusion
  131.2 2.1 fusion.3
  133.4 2.5 fusion.17
  136.8 1.2 slice-done.3
  138.0 6.7 %fusion.38 = f32[256,8192]{1,0:T(8,128)} fusion(bf16[1024,8192]{1,0:T(8,128)(2,1)S(1)} %bitcast.101, bf16[32,8,8,128]{3,2,1,0:T(8,128)(2,1)S(1)} %bitcast.109), kind=kOutput, calls=%fused_computation.40 | convolution fusion | flops 4294967296 | bytes 25690112 | tf_op jit(solution)/shard_map/dot_general | solution.py:128
  144.8 147.8 %reduce-scatter.2.cloned.1.call-done = f32[256,1024]{1,0:T(8,128)} async-done(((f32[256,8192]{1,0:T(8,128)}), f32[256,1024]{1,0:T(8,128)}) %reduce-scatter.2.cloned.1.call-update) | async-done | bytes 1048592 | tf_op jit(solution)/shard_map/reduce_scatter | solution.py:129
  292.6 2.1 convert_element_type.67
  295.2 7.7 %all-gather.5.cloned.1.call-done = bf16[512,1024]{1,0:T(8,128)(2,1)} async-done(((bf16[256,1024]{1,0:T(8,128)(2,1)}), bf16[512,1024]{1,0:T(8,128)(2,1)}) %all-gather.5.cloned.1.call-update) | async-done | bytes 1048592 | tf_op jit(solution)/shard_map/all_gather | solution.py:169
  302.9 1.8 gather_fusion.3
  304.7 1.0 fusion.37
  (70 shorter events, 8.7 us)
Async XLA Ops:
  6.5 99.5 %copy-start = (bf16[8192,128]{1,0:T(8,128)(2,1)S(1)}, bf16[8192,128]{1,0:T(8,128)(2,1)}, u32[]{:S(2)}) copy-start(bf16[8192,128]{1,0:T(8,128)(2,1)} %param.14) | copy-start | bytes 6291460
  6.5 96.4 %all-gather.3.cloned.1.call-start = ((), (), s32[]{:S(2)}) async-start(), calls=%async_computation.2 | async-start | bytes 4718592 | tf_op jit(solution)/shard_map/all_gather | solution.py:57
  11.1 49.9 %all-to-all-start = ((bf16[2,128,2,8,128]{4,1,0,2,3:T(8,128)(2,1)}), bf16[2,128,2,8,128]{4,1,0,2,3:T(8,128)(2,1)S(1)}, u32[]{:S(2)}, u32[]{:S(2)}) async-start(bf16[2,128,2,8,128]{4,1,0,2,3:T(8,128)(2,1)} %copy.87), calls=%async_computation | async-start | bytes 2097152 | tf_op jit(solution)/shard_map/all_to_all | solution.py:100
  18.4 274.1 %reduce-scatter.2.cloned.1.call-start = ((), (), s32[]{:S(2)}) async-start(), calls=%async_computation.3 | async-start | bytes 9437184 | tf_op jit(solution)/shard_map/reduce_scatter | solution.py:129
  62.1 48.2 %copy-start.6 = (f32[8192]{0:T(1024)S(1)}, f32[8192]{0:T(1024)}, u32[]{:S(2)}) copy-start(f32[8192]{0:T(1024)} %param.11) | copy-start | bytes 98308
  124.3 3.7 %copy-start.3 = (pred[128,128]{0,1:T(8,128)(4,1)S(1)}, pred[128,128]{0,1:T(8,128)(4,1)}, u32[]{:S(2)}) copy-start(pred[128,128]{0,1:T(8,128)(4,1)} %iota_compare_fusion) | copy-start | bytes 49156
  128.4 4.9 %copy-start.2 = (bf16[2,8,128,2,1,128]{5,2,1,0,3,4:T(8,128)(2,1)S(1)}, bf16[2,8,128,2,1,128]{5,2,1,0,3,4:T(8,128)(2,1)}, u32[]{:S(2)}) copy-start(bf16[2,8,128,2,1,128]{5,2,1,0,3,4:T(8,128)(2,1)} %copy.88) | copy-start | bytes 3145732
  131.2 5.4 %slice-start = ((s8[16777216]{0:T(1024)(128)(4,1)}), s8[4194304]{0:T(1024)(128)(4,1)S(1)}, s32[]{:S(2)}) async-start(s8[16777216]{0:T(1024)(128)(4,1)} %bitcast.100), calls=%async_computation.5 | async-start | bytes 8388608
  133.3 2.5 copy-start.4
  133.4 3.3 %slice-start.1 = ((s8[16777216]{0:T(1024)(128)(4,1)}), s8[4194304]{0:T(1024)(128)(4,1)S(1)}, s32[]{:S(2)}) async-start(s8[16777216]{0:T(1024)(128)(4,1)} %bitcast.100), calls=%async_computation.6 | async-start | bytes 8388608
  133.4 3.4 %slice-start.2 = ((s8[16777216]{0:T(1024)(128)(4,1)}), s8[4194304]{0:T(1024)(128)(4,1)S(1)}, s32[]{:S(2)}) async-start(s8[16777216]{0:T(1024)(128)(4,1)} %bitcast.100), calls=%async_computation.7 | async-start | bytes 8388608
  133.4 4.6 %slice-start.3 = ((s8[16777216]{0:T(1024)(128)(4,1)}), s8[4194304]{0:T(1024)(128)(4,1)S(1)}, s32[]{:S(2)}) async-start(s8[16777216]{0:T(1024)(128)(4,1)} %bitcast.100), calls=%async_computation.8 | async-start | bytes 8388608
  138.0 167.8 %copy-start.1 = (bf16[8192,128]{1,0:T(8,128)(2,1)S(1)}, bf16[8192,128]{1,0:T(8,128)(2,1)}, u32[]{:S(2)}) copy-start(bf16[8192,128]{1,0:T(8,128)(2,1)} %param.14) | copy-start | bytes 6291460
  144.7 150.0 %copy-start.5 = (s32[4]{0:T(128)S(1)}, s32[4]{0:T(128)}, u32[]{:S(2)}) copy-start(s32[4]{0:T(128)} %param.19) | copy-start | bytes 52
  144.7 158.1 %all-gather.5.cloned.1.call-start = ((), (), s32[]{:S(2)}) async-start(), calls=%async_computation.4 | async-start | bytes 1572864 | tf_op jit(solution)/shard_map/all_gather | solution.py:169
Sparse Core Ops, SparseCore 0:
  9.5 93.3 all-gather.2
  144.8 147.6 reduce-scatter.1
  294.8 8.0 all-gather.4
where the time goes:
time: 313 us; the launch traced here: 312 us
  waiting for transfers between devices  230 us (73%)
  matrix products  29.9 us (10%)
  local copies, waits for them, and re-layouts  19.5 us (6%)
  between operations  13.5 us (4%)
  other arithmetic  12.2 us (4%)
  starting transfers between devices  7.36 us (2%)
    reduce_scatter x1, waiting for transfers between devices, attend(): lax.psum_scatter(partial_value, 'tensor', scatter_dimension=1, tiled=True)  148 us
    all_gather x1, waiting for transfers between devices, attend(): lax.all_gather(token_rows, 'tensor', axis=1, tiled=True).astype(jnp.float32)  40.9 us
    all_to_all x1, waiting for transfers between devices, attend(): lax.all_to_all(spread, 'tensor', split_axis=3, concat_axis=1, tiled=True)  32.7 us
    dot_general x1, matrix products, attend(): jnp.dot(scaled, query_weight, preferred_element_type=jnp.float32)  9.52 us
    all_gather x1, waiting for transfers between devices, local(): everyone = lax.all_gather(mixed, 'worker', axis=0, tiled=True)  7.71 us
    all_to_all x1, starting transfers between devices, attend(): lax.all_to_all(spread, 'tensor', split_axis=3, concat_axis=1, tiled=True)  7.28 us
    dot_general x1, matrix products, attend(): jnp.dot(attended_rows, output_weight, preferred_element_type=jnp.float32)  6.74 us
  transfers between devices with their start and end apart: 4, of which 4 were waited for; matrix products, arithmetic and copies ran while one was open for 5% of the time, Pallas kernels for 0%

commit v1 on v0

v1 whole, which is shorter than its diff:
```python
import functools
import math

import jax
import jax.numpy as jnp
from jax import lax
from jax.experimental import pallas as pl
from jax.experimental.pallas import tpu as pltpu
from jax.sharding import PartitionSpec as P

HD = 128
NEW = 128
BLK = 16
CAP = 3
KVH = 8

MESH = pl.DeviceIdType.MESH
epsilon = 1e-05


def snake_order(count):
    def position(index):
        column, row = lax.rem(index, 2), lax.div(index, 2)
        return row + column * (count - 1 - 2 * row)

    def index(place):
        second = lax.div(place, count // 2)
        return second * (2 * (count - 1 - place) + 1) + (1 - second) * (2 * place)

    return position, index


def ring_order(mesh):
    devices = mesh.devices[0, 0]
    count = devices.shape[0]
    places = [getattr(device, "coords", None) for device in devices]
    if count > 2 and count % 2 == 0 and all(place is not None for place in places):
        ring = list(range(0, count, 2)) + list(range(count - 1, 0, -2))
        steps = [
            sum(abs(a - b) for a, b in zip(places[ring[k]], places[ring[(k + 1) % count]]))
            for k in range(count)
        ]
        if max(steps) == 1:
            return snake_order(count)
    return (lambda index: index), (lambda place: place)


def project_kernel(
    order, tok, gain, cosine, sine, wq, wk, wv, kvt,
    q_out, k_out, v_out, ctx,
    xg, wq_all, wk_all, wv_all, qacc, kacc, vacc, squares,
    weight_sem, send_sem, recv_sem, old_send, old_recv, own_sem,
):
    position, index = order
    n = xg.shape[0]
    half, part = xg.shape[3], xg.shape[4]
    width = 2 * part
    share = n // kvt.shape[0]
    me = lax.axis_index("tensor")
    place = position(me)
    forward = index(lax.rem(place + 1, n))
    back = index(lax.rem(place + n - 1, n))
    targets = (forward, back)
    streams = [(d, c) for c in range(2) for d in range(2)]

    def weight_copies(block):
        rows = pl.ds(pl.multiple_of(block * width, width), width)
        return [
            pltpu.make_async_copy(src.at[rows, :], dst.at[block], weight_sem.at[block, k])
            for k, (src, dst) in enumerate(((wq, wq_all), (wk, wk_all), (wv, wv_all)))
        ]

    def start_weights(k, carry):
        for copy in weight_copies(index(lax.rem(place + k, n))):
            copy.start()
        return carry

    def wait_weights(k, carry):
        for copy in weight_copies(index(lax.rem(place + k, n))):
            copy.wait()
        return carry

    barrier = pltpu.get_barrier_semaphore()

    def greet(k, carry):
        pl.semaphore_signal(
            barrier, inc=1, device_id={"tensor": lax.rem(me + k, n)}, device_id_type=MESH
        )
        return carry

    lax.fori_loop(1, n, greet, 0)
    lax.fori_loop(0, n, start_weights, 0)
    own = pltpu.make_async_copy(kvt.at[lax.div(me, share)], ctx.at[me], own_sem)
    own.start()
    for d, c in streams:
        xg[0, d, c] = tok[d * half : (d + 1) * half, c * part : (c + 1) * part]
    qacc[...] = jnp.zeros_like(qacc)
    kacc[...] = jnp.zeros_like(kacc)
    vacc[...] = jnp.zeros_like(vacc)
    squares[...] = jnp.zeros_like(squares)
    pl.semaphore_wait(barrier, n - 1)

    def hop(step, d, c):
        return pltpu.make_async_remote_copy(
            src_ref=xg.at[step, d, c],
            dst_ref=xg.at[step + 1, d, c],
            send_sem=send_sem.at[step, d, c],
            recv_sem=recv_sem.at[step + 1, d, c],
            device_id={"tensor": targets[d]},
            device_id_type=MESH,
        )

    def arrival(step, d, c):
        return pltpu.make_async_remote_copy(
            src_ref=xg.at[step, d, c],
            dst_ref=xg.at[step, d, c],
            send_sem=send_sem.at[step, d, c],
            recv_sem=recv_sem.at[step, d, c],
            device_id={"tensor": targets[d]},
            device_id_type=MESH,
        )

    def stored(k):
        target = lax.rem(me + k, n)
        return pltpu.make_async_remote_copy(
            src_ref=kvt.at[lax.div(target, share)],
            dst_ref=ctx.at[me],
            send_sem=old_send.at[k],
            recv_sem=old_recv.at[k],
            device_id={"tensor": target},
            device_id_type=MESH,
        )

    def stored_arrival(k):
        source = lax.rem(me + n - k, n)
        return pltpu.make_async_remote_copy(
            src_ref=kvt.at[0],
            dst_ref=ctx.at[source],
            send_sem=old_send.at[k],
            recv_sem=old_recv.at[k],
            device_id={"tensor": source},
            device_id_type=MESH,
        )

    def step_body(step, carry):
        blocks = (
            index(lax.rem(place + n - step, n)),
            index(lax.rem(place + step, n)),
        )
        for number, (d, c) in enumerate(streams):

            @pl.when(step > 0)
            def _():
                arrival(step, d, c).wait_recv()

            @pl.when(step < n - 1)
            def _():
                hop(step, d, c).start()

            if number == 0:

                @pl.when(step < n - 1)
                def _():
                    stored(step + 1).start()

                @pl.when(step == 0)
                def _():
                    wait_weights(0, 0)

                @pl.when(step == 1)
                def _():
                    lax.fori_loop(1, n, wait_weights, 0)

            block = blocks[d]
            values = xg[step, d, c].astype(jnp.float32)
            squares[d] += jnp.sum(values * values, axis=1, keepdims=True)
            offset = pl.multiple_of(block * width + c * part, part)
            scaled = (values * gain[:, pl.ds(offset, part)]).astype(jnp.bfloat16)
            rows = slice(c * part, (c + 1) * part)
            for total, weight in ((qacc, wq_all), (kacc, wk_all), (vacc, wv_all)):
                total[d] += jnp.dot(
                    scaled, weight[block, rows, :], preferred_element_type=jnp.float32
                )
        return carry

    lax.fori_loop(0, n, step_body, 0)

    for d in range(2):
        lines = slice(d * half, (d + 1) * half)
        factor = lax.rsqrt(squares[d] / (n * width) + epsilon)
        k_out[lines, :] = (kacc[d] * factor).astype(jnp.bfloat16)
        v_out[lines, :] = (vacc[d] * factor).astype(jnp.bfloat16)
        for head in range(q_out.shape[1] // HD):
            cols = slice(head * HD, (head + 1) * HD)
            query = qacc[d, :, cols] * factor
            turned = pltpu.roll(query, HD // 2, 1)
            q_out[lines, cols] = (query * cosine[lines, :] + turned * sine[lines, :]).astype(
                jnp.bfloat16
            )

    def finish(step, carry):
        for d, c in streams:
            hop(step, d, c).wait_send()
        stored(step + 1).wait_send()
        stored_arrival(step + 1).wait_recv()
        return carry

    lax.fori_loop(0, n - 1, finish, 0)
    own.wait()


def project(order, n, tokens, gain, cosine, sine, wq, wk, wv, kvt):
    rows, width = tokens.shape
    half, part = rows // 2, width // 2
    cols, narrow = wq.shape[1], wk.shape[1]
    vmem = pl.BlockSpec(memory_space=pltpu.VMEM)
    anywhere = pl.BlockSpec(memory_space=pl.ANY)
    return pl.pallas_call(
        functools.partial(project_kernel, order),
        out_shape=(
            jax.ShapeDtypeStruct((rows, cols), jnp.bfloat16),
            jax.ShapeDtypeStruct((rows, narrow), jnp.bfloat16),
            jax.ShapeDtypeStruct((rows, narrow), jnp.bfloat16),
            jax.ShapeDtypeStruct((n,) + kvt.shape[1:], jnp.bfloat16),
        ),
        in_specs=[vmem] * 4 + [anywhere] * 4,
        out_specs=(vmem, vmem, vmem, anywhere),
        scratch_shapes=[
            pltpu.VMEM((n, 2, 2, half, part), jnp.bfloat16),
            pltpu.VMEM((n, width, cols), jnp.bfloat16),
            pltpu.VMEM((n, width, narrow), jnp.bfloat16),
            pltpu.VMEM((n, width, narrow), jnp.bfloat16),
            pltpu.VMEM((2, half, cols), jnp.float32),
            pltpu.VMEM((2, half, narrow), jnp.float32),
            pltpu.VMEM((2, half, narrow), jnp.float32),
            pltpu.VMEM((2, half, 1), jnp.float32),
            pltpu.SemaphoreType.DMA((n, 3)),
            pltpu.SemaphoreType.DMA((n, 2, 2)),
            pltpu.SemaphoreType.DMA((n, 2, 2)),
            pltpu.SemaphoreType.DMA((n,)),
            pltpu.SemaphoreType.DMA((n,)),
            pltpu.SemaphoreType.DMA,
        ],
        compiler_params=pltpu.CompilerParams(
            collective_id=0, has_side_effects=True, vmem_limit_bytes=48 * 2**20
        ),
        name="gather_project",
    )(tokens, gain, cosine, sine, wq, wk, wv, kvt)


def attend_kernel(query, old, key_raw, value, cosine, sine, bias, mixture, key_turned):
    @pl.when(pl.program_id(1) == 0)
    def _():
        raw = key_raw[...].astype(jnp.float32)
        turned = pltpu.roll(raw, HD // 2, 1)
        key_turned[...] = (raw * cosine[...] + turned * sine[...]).astype(jnp.bfloat16)

    count = old.shape[0] * old.shape[3]
    old_key = old[:, 0, 0].reshape(count, HD)
    old_value = old[:, 0, 1].reshape(count, HD)
    inverse_root = 1.0 / math.sqrt(HD)
    across = (((1,), (1,)), ((), ()))
    old_scores = lax.dot_general(
        query[...], old_key, across, preferred_element_type=jnp.float32
    )
    new_scores = lax.dot_general(
        query[...], key_turned[...], across, preferred_element_type=jnp.float32
    )
    old_scores = jnp.where(bias[0] > 0, old_scores * inverse_root, -1e30)
    row = lax.broadcasted_iota(jnp.int32, new_scores.shape, 0)
    col = lax.broadcasted_iota(jnp.int32, new_scores.shape, 1)
    new_scores = jnp.where(row >= col, new_scores * inverse_root, -1e30)
    largest = jnp.maximum(
        jnp.max(old_scores, axis=1, keepdims=True), jnp.max(new_scores, axis=1, keepdims=True)
    )
    old_expo = jnp.exp(old_scores - largest)
    new_expo = jnp.exp(new_scores - largest)
    scale = 1.0 / (
        jnp.sum(old_expo, axis=1, keepdims=True) + jnp.sum(new_expo, axis=1, keepdims=True)
    )
    old_probs = (old_expo * scale).astype(jnp.bfloat16)
    new_probs = (new_expo * scale).astype(jnp.bfloat16)
    mixed = jnp.dot(old_probs, old_value, preferred_element_type=jnp.float32)
    mixed += jnp.dot(new_probs, value[...], preferred_element_type=jnp.float32)
    mixture[...] = mixed.astype(jnp.bfloat16)


def attention(query, old, key_raw, value, cosine, sine, bias):
    seqs = old.shape[1]
    heads = query.shape[1] // HD
    per_seq = pl.BlockSpec((NEW, HD), lambda s, h: (s, 0))
    per_head = pl.BlockSpec((NEW, HD), lambda s, h: (s, h))
    return pl.pallas_call(
        attend_kernel,
        out_shape=jax.ShapeDtypeStruct(query.shape, jnp.bfloat16),
        grid=(seqs, heads),
        in_specs=[
            per_head,
            pl.BlockSpec((old.shape[0], 1) + old.shape[2:], lambda s, h: (0, s, 0, 0, 0)),
            per_seq,
            per_seq,
            per_seq,
            per_seq,
            pl.BlockSpec((1, 1, bias.shape[2]), lambda s, h: (s, 0, 0)),
        ],
        out_specs=per_head,
        scratch_shapes=[pltpu.VMEM((NEW, HD), jnp.bfloat16)],
        compiler_params=pltpu.CompilerParams(vmem_limit_bytes=48 * 2**20),
        name="attention",
    )(query, old, key_raw, value, cosine, sine, bias)


def output_kernel(
    order, mixture, weight, everyone,
    weight_all, outgoing, incoming,
    weight_sem, send_sem, recv_sem, swap_send, swap_recv,
):
    position, index = order
    n = incoming.shape[0]
    half, part = incoming.shape[3], incoming.shape[4]
    width = 2 * part
    me = lax.axis_index("tensor")
    worker = lax.axis_index("worker")
    workers = everyone.shape[0]
    place = position(me)
    forward = index(lax.rem(place + 1, n))
    back = index(lax.rem(place + n - 1, n))
    targets = (forward, back)
    streams = [(d, c) for c in range(2) for d in range(2)]

    barrier = pltpu.get_barrier_semaphore()
    for target in targets:
        pl.semaphore_signal(barrier, inc=1, device_id={"tensor": target}, device_id_type=MESH)
    for k in range(1, workers):
        pl.semaphore_signal(
            barrier,
            inc=1,
            device_id={"worker": lax.rem(worker + k, workers)},
            device_id_type=MESH,
        )

    def weight_copy(block):
        cols = pl.ds(pl.multiple_of(block * width, width), width)
        return pltpu.make_async_copy(
            weight.at[:, cols], weight_all.at[block], weight_sem.at[block]
        )

    def start_weights(k, carry):
        weight_copy(index(lax.rem(place + n - 1 - k, n))).start()

        @pl.when(k < n // 2 - 1)
        def _():
            weight_copy(index(lax.rem(place + 1 + k, n))).start()

        return carry

    lax.fori_loop(0, n // 2, start_weights, 0)
    weight_copy(me).start()
    for d, c in streams:
        incoming[0, d, c] = jnp.zeros((half, part), jnp.bfloat16)
    pl.semaphore_wait(barrier, 1 + workers)

    def hop(step, d, c):
        return pltpu.make_async_remote_copy(
            src_ref=outgoing.at[step, d, c],
            dst_ref=incoming.at[step + 1, d, c],
            send_sem=send_sem.at[step, d, c],
            recv_sem=recv_sem.at[step + 1, d, c],
            device_id={"tensor": targets[d]},
            device_id_type=MESH,
        )

    def arrival(step, d, c):
        return pltpu.make_async_remote_copy(
            src_ref=outgoing.at[step, d, c],
            dst_ref=incoming.at[step, d, c],
            send_sem=send_sem.at[step, d, c],
            recv_sem=recv_sem.at[step, d, c],
            device_id={"tensor": targets[d]},
            device_id_type=MESH,
        )

    def step_body(step, carry):
        blocks = (
            index(lax.rem(place + 2 * n - 1 - step, n)),
            index(lax.rem(place + 1 + step, n)),
        )

        @pl.when(step < n // 2)
        def _():
            weight_copy(blocks[0]).wait()

        @pl.when(step < n // 2 - 1)
        def _():
            weight_copy(blocks[1]).wait()

        @pl.when(step == n // 2)
        def _():
            weight_copy(me).wait()

        for d, c in streams:
            product = jnp.dot(
                mixture[d * half : (d + 1) * half, :],
                weight_all[blocks[d], :, c * part : (c + 1) * part],
                preferred_element_type=jnp.float32,
            )

            @pl.when(step > 0)
            def _():
                arrival(step, d, c).wait_recv()

            summed = product + incoming[step, d, c].astype(jnp.float32)
            outgoing[step, d, c] = summed.astype(jnp.bfloat16)

            @pl.when(step < n - 1)
            def _():
                hop(step, d, c).start()

        return carry

    lax.fori_loop(0, n, step_body, 0)

    swaps = []
    for d in range(2):
        lines = slice(d * half, (d + 1) * half)
        for c in range(2):
            everyone[worker, lines, c * part : (c + 1) * part] = outgoing[n - 1, d, c]
        for k in range(1, workers):
            swap = pltpu.make_async_remote_copy(
                src_ref=everyone.at[worker, pl.ds(d * half, half)],
                dst_ref=everyone.at[worker, pl.ds(d * half, half)],
                send_sem=swap_send.at[k, d],
                recv_sem=swap_recv.at[k, d],
                device_id={"worker": lax.rem(worker + k, workers)},
                device_id_type=MESH,
            )
            swap.start()
            swaps.append(swap)

    def finish(step, carry):
        for d, c in streams:
            hop(step, d, c).wait_send()
        return carry

    lax.fori_loop(0, n - 1, finish, 0)
    for swap in swaps:
        swap.wait()


def project_out(order, n, workers, mixture, weight):
    rows, depth = mixture.shape
    width = weight.shape[1] // n
    half, part = rows // 2, width // 2
    vmem = pl.BlockSpec(memory_space=pltpu.VMEM)
    return pl.pallas_call(
        functools.partial(output_kernel, order),
        out_shape=jax.ShapeDtypeStruct((workers, rows, width), jnp.bfloat16),
        in_specs=[vmem, pl.BlockSpec(memory_space=pl.ANY)],
        out_specs=vmem,
        scratch_shapes=[
            pltpu.VMEM((n, depth, width), jnp.bfloat16),
            pltpu.VMEM((n, 2, 2, half, part), jnp.bfloat16),
            pltpu.VMEM((n, 2, 2, half, part), jnp.bfloat16),
            pltpu.SemaphoreType.DMA((n,)),
            pltpu.SemaphoreType.DMA((n, 2, 2)),
            pltpu.SemaphoreType.DMA((n, 2, 2)),
            pltpu.SemaphoreType.DMA((workers, 2)),
            pltpu.SemaphoreType.DMA((workers, 2)),
        ],
        compiler_params=pltpu.CompilerParams(
            collective_id=1, has_side_effects=True, vmem_limit_bytes=48 * 2**20
        ),
        name="project_out",
    )(mixture, weight)


def from_partner(block, axis, bit):
    count = lax.axis_size(axis)
    route = []
    for low in range(count):
        high = low | 1 << bit
        if high != low and high < count:
            route += [(low, high), (high, low)]
    return lax.ppermute(block, axis, route)


def whole_head(block, bits):
    me = lax.axis_index("tensor")
    for bit in range(bits):
        other = from_partner(block, "tensor", bit)
        upper = me // (1 << bit) % 2 == 1
        block = jnp.where(
            upper,
            jnp.concatenate([other, block], axis=1),
            jnp.concatenate([block, other], axis=1),
        )
    return block


def local(
    order,
    tokens,
    norm_gain,
    query_weight,
    key_weight,
    value_weight,
    output_weight,
    cached_blocks,
    cache_length,
    block_table,
    destination,
):
    n = lax.axis_size("tensor")
    workers = lax.axis_size("worker")
    worker_index = lax.axis_index("worker")
    seq_total = destination.shape[0]
    seqs, stored = cached_blocks.shape[0], cached_blocks.shape[1]
    lengths = lax.dynamic_slice_in_dim(cache_length, worker_index * seqs, seqs, 0)
    tables = lax.dynamic_slice_in_dim(block_table, worker_index * seqs, seqs, 0)

    halfway = HD // 2
    inverse = 500000.0 ** (-(jnp.arange(halfway, dtype=jnp.float32) * 2.0 / HD))
    positions = (lengths[:, None] + jnp.arange(NEW, dtype=jnp.int32)[None, :]).astype(jnp.float32)
    angles = positions.reshape(seqs * NEW, 1) * jnp.concatenate([inverse, inverse])[None, :]
    sign = jnp.where(jnp.arange(HD) < halfway, -1.0, 1.0)[None, :]
    cosine = jnp.cos(angles)
    sine = jnp.sin(angles) * sign

    logical = tables[:, :, None] * BLK + jnp.arange(BLK, dtype=jnp.int32)[None, None, :]
    seen = (logical < lengths[:, None, None]).astype(jnp.float32).reshape(seqs, 1, -1)

    kvt = cached_blocks.reshape(seqs, stored, 2, KVH, HD).transpose(3, 0, 2, 1, 4)
    query, key_raw, value, old = project(
        order, n, tokens, norm_gain[None, :], cosine, sine,
        query_weight, key_weight, value_weight, kvt,
    )
    bits = (n // KVH).bit_length() - 1
    key_raw, value = whole_head(key_raw, bits), whole_head(value, bits)
    mixture = attention(query, old, key_raw, value, cosine, sine, seen)
    everyone = project_out(order, n, workers, mixture, output_weight)
    everyone = everyone.reshape(seq_total, NEW, -1)

    belongs = destination == worker_index
    ranking = jnp.cumsum(belongs.astype(jnp.int32)) - 1
    result = jnp.zeros((CAP,) + everyone.shape[1:], everyone.dtype)
    slots = jnp.arange(CAP, dtype=jnp.int32)
    for seq in range(seq_total):
        chosen = belongs[seq] & (ranking[seq] == slots)
        result = jnp.where(chosen[:, None, None], everyone[seq][None], result)
    return result[None]


def solution(mesh):
    placed = (
        P(("groups", "worker"), "tensor"),
        P(),
        P(None, "tensor"),
        P(None, "tensor"),
        P(None, "tensor"),
        P("tensor", None),
        P(("groups", "worker"), "tensor", None, None),
        P("groups"),
        P("groups", None),
        P("groups"),
    )
    return jax.shard_map(
        functools.partial(local, ring_order(mesh)),
        mesh=mesh,
        in_specs=placed,
        out_specs=P(("groups", "worker"), None, None, "tensor"),
        check_vma=False,
    )
```

time: 313 us -> 146 us (0.47)
  waiting for transfers between devices: 230 us -> 0 us
  Pallas kernels: 0 us -> 129 us
  matrix products: 29.9 us -> 0 us
  between operations: 13.5 us -> 0.13 us
  local copies, waits for them, and re-layouts: 19.5 us -> 8.93 us
  starting transfers between devices: 7.36 us -> 0 us
  other arithmetic: 12.2 us -> 6.97 us
    reduce_scatter x1 -> x0, waiting for transfers between devices: 148 us -> none  [attend(): lax.psum_scatter(partial_value, 'tensor', scatter_dimension=1, tiled=True)]
    pallas_call x0 -> x3, Pallas kernels: none -> 129 us  [the longest x1 69.2 us: project(): pl.pallas_call(functools.partial(project_kernel, order), out_shape=(jax.S...]
    all_gather x2 -> x0, waiting for transfers between devices: 48.6 us -> none  [the longest x1 40.9 us: attend(): lax.all_gather(token_rows, 'tensor', axis=1, tiled=True).astype(jnp.float32)]
    all_to_all x1 -> x0, waiting for transfers between devices: 32.7 us -> none  [attend(): lax.all_to_all(spread, 'tensor', split_axis=3, concat_axis=1, tiled=True)]
    dot_general x8 -> x0, matrix products: 29.9 us -> none  [the longest x1 9.52 us: attend(): jnp.dot(scaled, query_weight, preferred_element_type=jnp.float32)]
    gather x5 -> x0, local copies, waits for them, and re-layouts: 9.63 us -> none  [the longest x2 5.26 us: attend(): logical = jnp.take(tables, stored // BLK, axis=1) * BLK + stored % BLK]
    all_to_all x1 -> x0, starting transfers between devices: 7.28 us -> none  [attend(): lax.all_to_all(spread, 'tensor', split_axis=3, concat_axis=1, tiled=True)]
    reduce_sum x4 -> x0, other arithmetic: 5.49 us -> none  [the longest x1 3.1 us: attend(): squares = jnp.sum(widened * widened, axis=1)]
  transfers between devices with their start and end apart: 4 -> 0, of which waited for: 4 -> 0; matrix products, arithmetic and copies ran while one was open for 5% -> 0% of each run, Pallas kernels for 0% -> 0%
where the time goes in v1:
time: 146 us; the launch traced here: 145 us
  Pallas kernels  129 us (88%)
  local copies, waits for them, and re-layouts  8.93 us (6%)
  other arithmetic  6.97 us (5%)
    pallas_call x1, Pallas kernels, project(): pl.pallas_call(functools.partial(project_kernel, order), out_shape=(jax.S...  69.2 us
    pallas_call x1, Pallas kernels, project_out(): pl.pallas_call(functools.partial(output_kernel, order), out_shape=jax.Sha...  48.2 us
    pallas_call x1, Pallas kernels, attention(): pl.pallas_call(attend_kernel, out_shape=jax.ShapeDtypeStruct(query.shape,...  11.9 us
    unnamed x11, local copies, waits for them, and re-layouts  5.95 us
    and x2, other arithmetic, local(): chosen = belongs[seq] & (ranking[seq] == slots)  4.9 us

profile of v1, /device:TPU:0, one launch (start us, length us, event | category | flops | bytes accessed | tf_op | source)
XLA Modules:
  0.0 145.2 jit_solution(10677130473590902826)
XLA Ops:
  0.0 0.7 dynamic_slice.6
  0.7 0.1 convert_bitcast_fusion
  0.8 0.1 compare_select_fusion
  0.9 0.5 fusion
  1.5 2.6 %copy.14 = bf16[2,128,2,1024]{1,3,2,0:T(8,128)(2,1)S(1)} copy(bf16[2,128,2,1024]{3,2,1,0:T(2,128)(2,1)} %param.16) | data formatting | bytes 2097152 | tf_op args[6]
  4.0 0.7 copy.15
  4.7 1.6 %copy-done = bf16[8192,128]{1,0:T(8,128)(2,1)S(1)} copy-done((bf16[8192,128]{1,0:T(8,128)(2,1)S(1)}, bf16[8192,128]{1,0:T(8,128)(2,1)}, u32[]{:S(2)}) %copy-start) | copy-done | bytes 2097176
  6.3 1.0 copy-done.1
  7.3 0.8 copy-done.2
  8.1 69.2 %gather_project.1 = (bf16[256,1024]{1,0:T(8,128)(2,1)S(1)}, bf16[256,128]{1,0:T(8,128)(2,1)S(1)}, bf16[256,128]{1,0:T(8,128)(2,1)S(1)}, bf16[8,2,2,128,128]{4,3,2,1,0:T(8,128)(2,1)S(1)}) custom-call(bf16[256,1024]{1,0:T(8,128)(2,1)S(1)} %copy-done.1, f32[1,8192]{1,0:T(1,128)S(1)} %bitcast.26, f32[256,128]{1,0:T(8,128)S(1)} %get-tuple-element.20.cosine, ...), custom_call_target="tpu_custom_call" | custom-call | tf_op jit(solution)/shard_map/gather_project/pallas_call | solution.py:218
  77.3 0.0 copy-start.4
  77.3 0.1 add.54
  77.4 0.1 add.60
  77.5 0.1 add.57
  77.6 0.1 compare_convert_fusion.bias
  77.7 11.9 %attention.1.mixture = bf16[256,1024]{1,0:T(8,128)(2,1)S(1)} custom-call(bf16[256,1024]{1,0:T(8,128)(2,1)S(1)} %get-tuple-element.9.query, bf16[8,2,2,128,128]{4,3,2,1,0:T(8,128)(2,1)S(1)} %get-tuple-element.10.old, bf16[256,128]{1,0:T(8,128)(2,1)S(1)} %get-tuple-element.11.key_raw, bf16[256,128]{1,0:T(8,128)(2,1)S(1)} %get-tuple-element.12.value, ...), custom_call_target="tpu_custom_call" | custom-call | tf_op jit(solution)/shard_map/attention/pallas_call | solution.py:293
  89.5 48.2 %project_out.1 = bf16[2,256,1024]{2,1,0:T(8,128)(2,1)S(1)} custom-call(bf16[256,1024]{1,0:T(8,128)(2,1)S(1)} %attention.1.mixture, bf16[1024,8192]{1,0:T(8,128)(2,1)} %weight.1), custom_call_target="tpu_custom_call" | custom-call | tf_op jit(solution)/shard_map/project_out/pallas_call | solution.py:455
  137.7 0.1 slice_bitcast_fusion.3
  137.8 0.2 reduce-window.9
  138.0 0.6 fusion.1
  138.6 0.6 fusion.2
  139.2 2.5 %compare_and_fusion.2 = (pred[3]{0:T(512)(128)(4,1)S(1)}, pred[3]{0:T(512)(128)(4,1)S(1)}) fusion(pred[]{:T(512)} %bitcast.9, s32[]{:T(128)} %bitcast.10, s32[]{:T(128)} %bitcast.2, pred[]{:T(512)} %bitcast), kind=kLoop, calls=%fused_computation.11 | loop fusion | flops 12 | bytes 16 | tf_op jit(solution)/shard_map/and | solution.py:548
  141.7 2.4 %compare_and_fusion = (pred[3]{0:T(512)(128)(4,1)S(1)}, pred[3]{0:T(512)(128)(4,1)S(1)}) fusion(pred[]{:T(512)} %bitcast.15, s32[]{:T(128)} %bitcast.16, s32[]{:T(128)} %bitcast.13, pred[]{:T(512)} %bitcast.12), kind=kLoop, calls=%fused_computation.9 | loop fusion | flops 12 | bytes 16 | tf_op jit(solution)/shard_map/and | solution.py:548
  144.1 1.1 select_select_fusion
  (11 shorter events, 0.1 us)
Async XLA Ops:
  0.0 77.3 %copy-start.3 = (s32[4,64]{1,0:T(4,128)S(1)}, s32[4,64]{1,0:T(4,128)}, u32[]{:S(2)}) copy-start(s32[4,64]{1,0:T(4,128)} %param.18) | copy-start | bytes 3076
  4.7 1.6 %copy-start = (bf16[8192,128]{1,0:T(8,128)(2,1)S(1)}, bf16[8192,128]{1,0:T(8,128)(2,1)}, u32[]{:S(2)}) copy-start(bf16[8192,128]{1,0:T(8,128)(2,1)} %wk.1) | copy-start | bytes 6291460
  6.3 1.0 copy-start.1
  7.3 0.8 copy-start.2
  77.3 60.5 %copy-start.4 = (s32[4]{0:T(128)S(1)}, s32[4]{0:T(128)}, u32[]{:S(2)}) copy-start(s32[4]{0:T(128)} %param.19) | copy-start | bytes 52

commit v2 on v1

v2 whole, which is shorter than its diff:
```python
import functools
import math

import jax
import jax.numpy as jnp
import numpy as np
from jax import lax
from jax.experimental import pallas as pl
from jax.experimental.pallas import tpu as pltpu
from jax.sharding import PartitionSpec as P

HD = 128
NEW = 128
BLK = 16
CAP = 3
KVH = 8

MESH = pl.DeviceIdType.MESH
epsilon = 1e-05


def snake_order(count):
    def position(index):
        column, row = lax.rem(index, 2), lax.div(index, 2)
        return row + column * (count - 1 - 2 * row)

    def index(place):
        second = lax.div(place, count // 2)
        return second * (2 * (count - 1 - place) + 1) + (1 - second) * (2 * place)

    return position, index


def layout(mesh):
    devices = mesh.devices[0, 0]
    count = devices.shape[0]
    places = [getattr(device, "coords", None) for device in devices]
    if count > 2 and count % 2 == 0 and all(place is not None for place in places):
        ring = list(range(0, count, 2)) + list(range(count - 1, 0, -2))
        steps = [
            sum(abs(a - b) for a, b in zip(places[ring[k]], places[ring[(k + 1) % count]]))
            for k in range(count)
        ]
        if max(steps) == 1:
            return snake_order(count), (count // 2, 2, False)
    return ((lambda index: index), (lambda place: place)), (count, 1, True)


def project_kernel(
    grid, seqs, tok, gain_hbm, inverse, lengths, wq, wk, wv, cached,
    q_out, k_out, v_out, cosine, sine, ctx,
    xg, gain, raw, kvt, wq_all, wk_all, wv_all, qacc, kacc, vacc, squares,
    weight_sem, send_sem, recv_sem, old_send, old_recv, own_sem, load_sem,
):
    lines, columns, wraps = grid
    n, parts, rows, part = xg.shape
    width = parts * part
    share = n // kvt.shape[0]
    me = lax.axis_index("tensor")
    worker = lax.axis_index("worker")
    line, column = lax.div(me, columns), lax.rem(me, columns)
    other = columns - 1 - column
    reach = lines // 2 + 1 if wraps else lines

    def source(k, side, where):
        moved = line + lines + (2 * side - 1) * k
        return lax.rem(moved, lines) * columns + where

    def comes(k, side):
        if wraps:
            return k + side <= lines // 2
        from_below = (1 - side) * (line - k)
        from_above = side * (lines - 1 - line - k)
        return from_below + from_above >= 0

    def goes_on(k, side):
        if wraps:
            return k + side < lines // 2
        return (1 - side) * (lines - 1 - line) + side * line > 0

    def neighbour(side):
        return lax.rem(line + lines + 1 - 2 * side, lines) * columns + column

    across = line * columns + other

    def weight_copies(block):
        span = pl.ds(pl.multiple_of(block * width, width), width)
        return [
            pltpu.make_async_copy(src.at[span, :], dst.at[block], weight_sem.at[block, k])
            for k, (src, dst) in enumerate(((wq, wq_all), (wk, wk_all), (wv, wv_all)))
        ]

    def start_weights(block):
        for copy in weight_copies(block):
            copy.start()

    barrier = pltpu.get_barrier_semaphore()

    def greet(k, carry):
        pl.semaphore_signal(
            barrier, inc=1, device_id={"tensor": lax.rem(me + k, n)}, device_id_type=MESH
        )
        return carry

    lax.fori_loop(1, n, greet, 0)

    def own_part(c):
        span = pl.ds(pl.multiple_of(c * part, part), part)
        return tok.at[:, span]

    own_parts = [
        pltpu.make_async_copy(own_part(c), xg.at[me, c], load_sem.at[c]) for c in range(parts)
    ]
    for copy in own_parts:
        copy.start()
    load_gain = pltpu.make_async_copy(gain_hbm, gain, load_sem.at[parts])
    load_gain.start()
    load_cached = pltpu.make_async_copy(cached, raw, load_sem.at[parts + 1])
    load_cached.start()
    start_weights(me)

    def spread(k, carry):
        for side in range(2):

            @pl.when(comes(k, side))
            def _():
                start_weights(source(k, side, column))

        return carry

    lax.fori_loop(1, reach, spread, 0)
    pl.semaphore_wait(barrier, n - 1)

    def remote(src, block, c, way, target):
        return pltpu.make_async_remote_copy(
            src_ref=src,
            dst_ref=xg.at[block, c],
            send_sem=send_sem.at[way, block, c],
            recv_sem=recv_sem.at[block, c],
            device_id={"tensor": target},
            device_id_type=MESH,
        )

    def own_hops(c):
        hops = [(goes_on(0, side), remote(own_part(c), me, c, side, neighbour(side))) for side in range(2)]
        if columns > 1:
            hops.append((True, remote(own_part(c), me, c, 2, across)))
        return hops

    for c in range(parts):
        for needed, copy in own_hops(c):
            pl.when(needed)(copy.start)

    def onward(k, side, block, c):
        hops = [(goes_on(k, side), remote(xg.at[block, c], block, c, side, neighbour(side)))]
        if columns > 1:
            hops.append((True, remote(xg.at[block, c], block, c, 2, across)))
        return hops

    def spread_across(k, carry):
        for side in range(2):

            @pl.when(comes(k, side) & (k + 1 > side))
            def _():
                start_weights(source(k, side, other))

        return carry

    if columns > 1:
        start_weights(across)
        lax.fori_loop(1, reach, spread_across, 0)

    load_cached.wait()
    for seq in range(raw.shape[0]):
        for kind in range(2):
            for head in range(kvt.shape[0]):
                kvt[head, seq, kind] = raw[seq, :, kind, head * HD : (head + 1) * HD]

    def stored(k):
        target = lax.rem(me + k, n)
        return pltpu.make_async_remote_copy(
            src_ref=kvt.at[lax.div(target, share)],
            dst_ref=ctx.at[me],
            send_sem=old_send.at[k],
            recv_sem=old_recv.at[k],
            device_id={"tensor": target},
            device_id_type=MESH,
        )

    def stored_arrival(k):
        origin = lax.rem(me + n - k, n)
        return pltpu.make_async_remote_copy(
            src_ref=kvt.at[0],
            dst_ref=ctx.at[origin],
            send_sem=old_send.at[k],
            recv_sem=old_recv.at[k],
            device_id={"tensor": origin},
            device_id_type=MESH,
        )

    own = pltpu.make_async_copy(kvt.at[lax.div(me, share)], ctx.at[me], own_sem)
    own.start()
    each = -(-(n - 1) // reach)

    def send_stored(k):
        for extra in range(each):
            number = 1 + k * each + extra

            @pl.when(number < n)
            def _():
                stored(number).start()

    qacc[...] = jnp.zeros_like(qacc)
    kacc[...] = jnp.zeros_like(kacc)
    vacc[...] = jnp.zeros_like(vacc)
    squares[...] = jnp.zeros_like(squares)

    def multiply(block, c):
        @pl.when(c == 0)
        def _():
            for copy in weight_copies(block):
                copy.wait()

        values = xg[block, c].astype(jnp.float32)
        squares[...] += jnp.sum(values * values, axis=1, keepdims=True)
        offset = pl.multiple_of(block * width + c * part, part)
        scaled = (values * gain[:, pl.ds(offset, part)]).astype(jnp.bfloat16)
        span = pl.ds(pl.multiple_of(c * part, part), part)
        for total, weight in ((qacc, wq_all), (kacc, wk_all), (vacc, wv_all)):
            total[...] += jnp.dot(
                scaled, weight[block, span, :], preferred_element_type=jnp.float32
            )

    load_gain.wait()
    for copy in own_parts:
        copy.wait()
    send_stored(0)

    def own_body(c, carry):
        multiply(me, c)
        return carry

    lax.fori_loop(0, parts, own_body, 0)

    for seq in range(seqs):
        span = slice(seq * NEW, (seq + 1) * NEW)
        start = lengths[worker * seqs + seq]
        position = start + lax.broadcasted_iota(jnp.int32, (NEW, HD), 0)
        angle = position.astype(jnp.float32) * inverse[...]
        lane = lax.broadcasted_iota(jnp.int32, (NEW, HD), 1)
        cosine[span, :] = jnp.cos(angle)
        turn = jnp.sin(angle)
        sine[span, :] = jnp.where(lane < HD // 2, -turn, turn)

    def arrive(block, c):
        remote(xg.at[block, c], block, c, 0, across).wait_recv()

    def along(k, carry):
        send_stored(k)

        def piece(number, carry):
            c, side = lax.div(number, 2), lax.rem(number, 2)
            block = source(k, side, column)

            @pl.when(comes(k, side))
            def _():
                arrive(block, c)
                for needed, copy in onward(k, side, block, c):
                    pl.when(needed)(copy.start)
                multiply(block, c)

            return carry

        return lax.fori_loop(0, 2 * parts, piece, carry)

    lax.fori_loop(1, reach, along, 0)

    def beyond(k, carry):
        def piece(number, carry):
            c, side = lax.div(number, 2), lax.rem(number, 2)
            block = source(k, side, other)

            @pl.when(comes(k, side) & (k + 1 > side))
            def _():
                arrive(block, c)
                multiply(block, c)

            return carry

        return lax.fori_loop(0, 2 * parts, piece, carry)

    if columns > 1:
        lax.fori_loop(0, reach, beyond, 0)

    factor = lax.rsqrt(squares[...] / (n * width) + epsilon)
    k_out[...] = (kacc[...] * factor).astype(jnp.bfloat16)
    v_out[...] = (vacc[...] * factor).astype(jnp.bfloat16)
    for head in range(q_out.shape[1] // HD):
        cols = slice(head * HD, (head + 1) * HD)
        query = qacc[:, cols] * factor
        turned = pltpu.roll(query, HD // 2, 1)
        q_out[:, cols] = (query * cosine[...] + turned * sine[...]).astype(jnp.bfloat16)

    for c in range(parts):
        for needed, copy in own_hops(c):
            pl.when(needed)(copy.wait_send)

    def sent(k, carry):
        def piece(number, carry):
            c, side = lax.div(number, 2), lax.rem(number, 2)
            block = source(k, side, column)

            @pl.when(comes(k, side))
            def _():
                for needed, copy in onward(k, side, block, c):
                    pl.when(needed)(copy.wait_send)

            return carry

        return lax.fori_loop(0, 2 * parts, piece, carry)

    lax.fori_loop(1, reach, sent, 0)

    def finish(k, carry):
        stored(k).wait_send()
        stored_arrival(k).wait_recv()
        return carry

    lax.fori_loop(1, n, finish, 0)
    own.wait()


def project(grid, n, tokens, gain, inverse, lengths, wq, wk, wv, cached):
    rows, width = tokens.shape
    part = max(HD, width // 4)
    parts = width // part
    cols, narrow = wq.shape[1], wk.shape[1]
    seqs, stored = cached.shape[0], cached.shape[1]
    vmem = pl.BlockSpec(memory_space=pltpu.VMEM)
    smem = pl.BlockSpec(memory_space=pltpu.SMEM)
    anywhere = pl.BlockSpec(memory_space=pl.ANY)
    kvt = (KVH, seqs, 2, stored, HD)
    ways = 2 + (grid[1] > 1)
    return pl.pallas_call(
        functools.partial(project_kernel, grid, seqs),
        out_shape=(
            jax.ShapeDtypeStruct((rows, cols), jnp.bfloat16),
            jax.ShapeDtypeStruct((rows, narrow), jnp.bfloat16),
            jax.ShapeDtypeStruct((rows, narrow), jnp.bfloat16),
            jax.ShapeDtypeStruct((rows, HD), jnp.float32),
            jax.ShapeDtypeStruct((rows, HD), jnp.float32),
            jax.ShapeDtypeStruct((n,) + kvt[1:], jnp.bfloat16),
        ),
        in_specs=[anywhere, anywhere, vmem, smem] + [anywhere] * 4,
        out_specs=(vmem,) * 5 + (anywhere,),
        scratch_shapes=[
            pltpu.VMEM((n, parts, rows, part), jnp.bfloat16),
            pltpu.VMEM(gain.shape, jnp.float32),
            pltpu.VMEM(cached.shape, jnp.bfloat16),
            pltpu.VMEM(kvt, jnp.bfloat16),
            pltpu.VMEM((n, width, cols), jnp.bfloat16),
            pltpu.VMEM((n, width, narrow), jnp.bfloat16),
            pltpu.VMEM((n, width, narrow), jnp.bfloat16),
            pltpu.VMEM((rows, cols), jnp.float32),
            pltpu.VMEM((rows, narrow), jnp.float32),
            pltpu.VMEM((rows, narrow), jnp.float32),
            pltpu.VMEM((rows, 1), jnp.float32),
            pltpu.SemaphoreType.DMA((n, 3)),
            pltpu.SemaphoreType.DMA((ways, n, parts)),
            pltpu.SemaphoreType.DMA((n, parts)),
            pltpu.SemaphoreType.DMA((n,)),
            pltpu.SemaphoreType.DMA((n,)),
            pltpu.SemaphoreType.DMA,
            pltpu.SemaphoreType.DMA((parts + 2,)),
        ],
        compiler_params=pltpu.CompilerParams(
            collective_id=0, has_side_effects=True, vmem_limit_bytes=60 * 2**20
        ),
        name="gather_project",
    )(tokens, gain, inverse, lengths, wq, wk, wv, cached)


def attend_kernel(query, old, key_raw, value, cosine, sine, bias, mixture, key_turned):
    @pl.when(pl.program_id(1) == 0)
    def _():
        raw = key_raw[...].astype(jnp.float32)
        turned = pltpu.roll(raw, HD // 2, 1)
        key_turned[...] = (raw * cosine[...] + turned * sine[...]).astype(jnp.bfloat16)

    heads = query.shape[1] // HD
    count = old.shape[0] * old.shape[3]
    old_key = old[:, 0, 0].reshape(count, HD)
    old_value = old[:, 0, 1].reshape(count, HD)
    scale = math.log2(math.e) / math.sqrt(HD)
    contract = (((1,), (1,)), ((), ()))
    seen = bias[0] > 0
    row = lax.broadcasted_iota(jnp.int32, (NEW, NEW), 0)
    col = lax.broadcasted_iota(jnp.int32, (NEW, NEW), 1)
    for head in range(heads):
        cols = slice(head * HD, (head + 1) * HD)
        one = query[:, cols]
        old_scores = lax.dot_general(one, old_key, contract, preferred_element_type=jnp.float32)
        new_scores = lax.dot_general(
            one, key_turned[...], contract, preferred_element_type=jnp.float32
        )
        old_scores = jnp.where(seen, old_scores * scale, -1e30)
        new_scores = jnp.where(row >= col, new_scores * scale, -1e30)
        largest = jnp.maximum(
            jnp.max(old_scores, axis=1, keepdims=True),
            jnp.max(new_scores, axis=1, keepdims=True),
        )
        old_expo = jnp.exp2(old_scores - largest)
        new_expo = jnp.exp2(new_scores - largest)
        inverse = 1.0 / (
            jnp.sum(old_expo, axis=1, keepdims=True) + jnp.sum(new_expo, axis=1, keepdims=True)
        )
        old_probs = (old_expo * inverse).astype(jnp.bfloat16)
        new_probs = (new_expo * inverse).astype(jnp.bfloat16)
        mixed = jnp.dot(old_probs, old_value, preferred_element_type=jnp.float32)
        mixed += jnp.dot(new_probs, value[...], preferred_element_type=jnp.float32)
        mixture[:, cols] = mixed.astype(jnp.bfloat16)


def attention(query, old, key_raw, value, cosine, sine, bias):
    seqs = old.shape[1]
    heads = query.shape[1] // HD
    together = math.gcd(heads, 4)
    per_seq = pl.BlockSpec((NEW, HD), lambda s, h: (s, 0))
    per_head = pl.BlockSpec((NEW, HD * together), lambda s, h: (s, h))
    return pl.pallas_call(
        attend_kernel,
        out_shape=jax.ShapeDtypeStruct(query.shape, jnp.bfloat16),
        grid=(seqs, heads // together),
        in_specs=[
            per_head,
            pl.BlockSpec((old.shape[0], 1) + old.shape[2:], lambda s, h: (0, s, 0, 0, 0)),
            per_seq,
            per_seq,
            per_seq,
            per_seq,
            pl.BlockSpec((1, 1, bias.shape[2]), lambda s, h: (s, 0, 0)),
        ],
        out_specs=per_head,
        scratch_shapes=[pltpu.VMEM((NEW, HD), jnp.bfloat16)],
        compiler_params=pltpu.CompilerParams(vmem_limit_bytes=48 * 2**20),
        name="attention",
    )(query, old, key_raw, value, cosine, sine, bias)


def output_kernel(
    order, mixture, weight, destination, result,
    everyone, weight_all, outgoing, incoming,
    weight_sem, send_sem, recv_sem, swap_send, swap_recv,
):
    position, index = order
    n = incoming.shape[0]
    half, part = incoming.shape[3], incoming.shape[4]
    width = 2 * part
    me = lax.axis_index("tensor")
    worker = lax.axis_index("worker")
    workers = everyone.shape[0]
    place = position(me)
    forward = index(lax.rem(place + 1, n))
    back = index(lax.rem(place + n - 1, n))
    targets = (forward, back)
    streams = [(d, c) for c in range(2) for d in range(2)]

    barrier = pltpu.get_barrier_semaphore()
    for target in targets:
        pl.semaphore_signal(barrier, inc=1, device_id={"tensor": target}, device_id_type=MESH)
    for k in range(1, workers):
        pl.semaphore_signal(
            barrier,
            inc=1,
            device_id={"worker": lax.rem(worker + k, workers)},
            device_id_type=MESH,
        )

    def weight_copy(block):
        cols = pl.ds(pl.multiple_of(block * width, width), width)
        return pltpu.make_async_copy(
            weight.at[:, cols], weight_all.at[block], weight_sem.at[block]
        )

    def start_weights(k, carry):
        weight_copy(index(lax.rem(place + n - 1 - k, n))).start()

        @pl.when(k < n // 2 - 1)
        def _():
            weight_copy(index(lax.rem(place + 1 + k, n))).start()

        return carry

    lax.fori_loop(0, n // 2, start_weights, 0)
    weight_copy(me).start()
    for d, c in streams:
        incoming[0, d, c] = jnp.zeros((half, part), jnp.bfloat16)
    pl.semaphore_wait(barrier, 1 + workers)

    def hop(step, d, c):
        return pltpu.make_async_remote_copy(
            src_ref=outgoing.at[step, d, c],
            dst_ref=incoming.at[step + 1, d, c],
            send_sem=send_sem.at[step, d, c],
            recv_sem=recv_sem.at[step + 1, d, c],
            device_id={"tensor": targets[d]},
            device_id_type=MESH,
        )

    def arrival(step, d, c):
        return pltpu.make_async_remote_copy(
            src_ref=outgoing.at[step, d, c],
            dst_ref=incoming.at[step, d, c],
            send_sem=send_sem.at[step, d, c],
            recv_sem=recv_sem.at[step, d, c],
            device_id={"tensor": targets[d]},
            device_id_type=MESH,
        )

    def step_body(step, carry):
        blocks = (
            index(lax.rem(place + 2 * n - 1 - step, n)),
            index(lax.rem(place + 1 + step, n)),
        )

        @pl.when(step < n // 2)
        def _():
            weight_copy(blocks[0]).wait()

        @pl.when(step < n // 2 - 1)
        def _():
            weight_copy(blocks[1]).wait()

        @pl.when(step == n // 2)
        def _():
            weight_copy(me).wait()

        for d, c in streams:
            product = jnp.dot(
                mixture[d * half : (d + 1) * half, :],
                weight_all[blocks[d], :, c * part : (c + 1) * part],
                preferred_element_type=jnp.float32,
            )

            @pl.when(step > 0)
            def _():
                arrival(step, d, c).wait_recv()

            summed = product + incoming[step, d, c].astype(jnp.float32)
            outgoing[step, d, c] = summed.astype(jnp.bfloat16)

            @pl.when(step < n - 1)
            def _():
                hop(step, d, c).start()

        return carry

    lax.fori_loop(0, n, step_body, 0)

    swaps = []
    for d in range(2):
        lines = slice(d * half, (d + 1) * half)
        for c in range(2):
            everyone[worker, lines, c * part : (c + 1) * part] = outgoing[n - 1, d, c]
        for k in range(1, workers):
            swap = pltpu.make_async_remote_copy(
                src_ref=everyone.at[worker, pl.ds(d * half, half)],
                dst_ref=everyone.at[worker, pl.ds(d * half, half)],
                send_sem=swap_send.at[k, d],
                recv_sem=swap_recv.at[k, d],
                device_id={"worker": lax.rem(worker + k, workers)},
                device_id_type=MESH,
            )
            swap.start()
            swaps.append(swap)

    def finish(step, carry):
        for d, c in streams:
            hop(step, d, c).wait_send()
        return carry

    lax.fori_loop(0, n - 1, finish, 0)
    for swap in swaps:
        swap.wait()

    seqs = destination.shape[0]
    local_seqs = seqs // workers
    bound = [jnp.where(destination[seq] == worker, 1, 0) for seq in range(seqs)]
    rank, ranks = 0, []
    for seq in range(seqs):
        ranks.append(rank)
        rank = rank + bound[seq]
    for slot in range(result.shape[0]):
        chosen = [jnp.where(ranks[seq] == slot, bound[seq], 0) for seq in range(seqs)]
        picked = jnp.zeros(result.shape[1:], result.dtype)
        for seq in range(seqs):
            first = seq % local_seqs * NEW
            rows = everyone[seq // local_seqs, first : first + NEW, :]
            flag = jnp.full(result.shape[1:], chosen[seq], jnp.int32)
            picked = jnp.where(flag > 0, rows, picked)
        result[slot] = picked


def project_out(order, n, workers, mixture, weight, destination):
    rows, depth = mixture.shape
    width = weight.shape[1] // n
    half, part = rows // 2, width // 2
    vmem = pl.BlockSpec(memory_space=pltpu.VMEM)
    return pl.pallas_call(
        functools.partial(output_kernel, order),
        out_shape=jax.ShapeDtypeStruct((CAP, NEW, width), jnp.bfloat16),
        in_specs=[
            vmem,
            pl.BlockSpec(memory_space=pl.ANY),
            pl.BlockSpec(memory_space=pltpu.SMEM),
        ],
        out_specs=vmem,
        scratch_shapes=[
            pltpu.VMEM((workers, rows, width), jnp.bfloat16),
            pltpu.VMEM((n, depth, width), jnp.bfloat16),
            pltpu.VMEM((n, 2, 2, half, part), jnp.bfloat16),
            pltpu.VMEM((n, 2, 2, half, part), jnp.bfloat16),
            pltpu.SemaphoreType.DMA((n,)),
            pltpu.SemaphoreType.DMA((n, 2, 2)),
            pltpu.SemaphoreType.DMA((n, 2, 2)),
            pltpu.SemaphoreType.DMA((workers, 2)),
            pltpu.SemaphoreType.DMA((workers, 2)),
        ],
        compiler_params=pltpu.CompilerParams(
            collective_id=1, has_side_effects=True, vmem_limit_bytes=48 * 2**20
        ),
        name="project_out",
    )(mixture, weight, destination)


def from_partner(block, axis, bit):
    count = lax.axis_size(axis)
    route = []
    for low in range(count):
        high = low | 1 << bit
        if high != low and high < count:
            route += [(low, high), (high, low)]
    return lax.ppermute(block, axis, route)


def whole_head(block, bits):
    me = lax.axis_index("tensor")
    for bit in range(bits):
        other = from_partner(block, "tensor", bit)
        upper = me // (1 << bit) % 2 == 1
        block = jnp.where(
            upper,
            jnp.concatenate([other, block], axis=1),
            jnp.concatenate([block, other], axis=1),
        )
    return block


def local(
    ring,
    grid,
    tokens,
    norm_gain,
    query_weight,
    key_weight,
    value_weight,
    output_weight,
    cached_blocks,
    cache_length,
    block_table,
    destination,
):
    n = lax.axis_size("tensor")
    workers = lax.axis_size("worker")
    seqs = cached_blocks.shape[0]
    first = lax.axis_index("worker") * seqs
    lengths = lax.dynamic_slice_in_dim(cache_length, first, seqs, 0)
    tables = lax.dynamic_slice_in_dim(block_table, first, seqs, 0)
    logical = tables[:, :, None] * BLK + jnp.arange(BLK, dtype=jnp.int32)[None, None, :]
    seen = (logical < lengths[:, None, None]).astype(jnp.float32).reshape(seqs, 1, -1)

    half = 500000.0 ** (-(np.arange(HD // 2) * 2.0 / HD))
    inverse = jnp.asarray(np.concatenate([half, half])[None, :], jnp.float32)
    query, key_raw, value, cosine, sine, old = project(
        grid, n, tokens, norm_gain[None, :], inverse, cache_length,
        query_weight, key_weight, value_weight, cached_blocks,
    )
    bits = (n // KVH).bit_length() - 1
    key_raw, value = whole_head(key_raw, bits), whole_head(value, bits)
    mixture = attention(query, old, key_raw, value, cosine, sine, seen)
    return project_out(ring, n, workers, mixture, output_weight, destination)[None]


def solution(mesh):
    placed = (
        P(("groups", "worker"), "tensor"),
        P(),
        P(None, "tensor"),
        P(None, "tensor"),
        P(None, "tensor"),
        P("tensor", None),
        P(("groups", "worker"), "tensor", None, None),
        P("groups"),
        P("groups", None),
        P("groups"),
    )
    return jax.shard_map(
        functools.partial(local, *layout(mesh)),
        mesh=mesh,
        in_specs=placed,
        out_specs=P(("groups", "worker"), None, None, "tensor"),
        check_vma=False,
    )
```

time: 146 us -> 134 us (0.918)
  other arithmetic: 6.97 us -> 0.76 us
  Pallas kernels: 129 us -> 125 us
    and x2 -> x0, other arithmetic: 4.9 us -> none  [local(): chosen = belongs[seq] & (ranking[seq] == slots)]
    pallas_call x1, Pallas kernels: 11.9 us -> 9.07 us  [attention(): pl.pallas_call(attend_kernel, out_shape=jax.ShapeDtypeStruct(query.shape,...]
    unnamed x11 -> x15, local copies, waits for them, and re-layouts: 5.95 us -> 6.63 us
where the time goes in v2:
time: 134 us; the launch traced here: 133 us
  Pallas kernels  125 us (93%)
  local copies, waits for them, and re-layouts  7.63 us (6%)
    pallas_call x1, Pallas kernels, project(): pl.pallas_call(functools.partial(project_kernel, grid, seqs), out_shape=(...  68.1 us
    pallas_call x1, Pallas kernels, project_out(): pl.pallas_call(functools.partial(output_kernel, order), out_shape=jax.Sha...  47.7 us
    pallas_call x1, Pallas kernels, attention(): pl.pallas_call(attend_kernel, out_shape=jax.ShapeDtypeStruct(query.shape,...  9.07 us
    unnamed x15, local copies, waits for them, and re-layouts  6.63 us

profile of v2, /device:TPU:0, one launch (start us, length us, event | category | flops | bytes accessed | tf_op | source)
XLA Modules:
  0.0 133.4 jit_solution(12904011781510505774)
XLA Ops:
  0.0 0.0 copy-start.6
  0.0 0.7 dynamic_slice.7
  0.7 0.7 dynamic-slice_multiply_fusion
  1.4 0.1 add.34
  1.5 0.1 add.31
  1.6 0.1 add.37
  1.7 0.1 compare_convert_fusion.bias
  1.8 68.1 %gather_project.1 = (bf16[256,1024]{1,0:T(8,128)(2,1)}, bf16[256,128]{1,0:T(8,128)(2,1)}, bf16[256,128]{1,0:T(8,128)(2,1)}, f32[256,128]{1,0:T(8,128)}, f32[256,...) custom-call(bf16[256,1024]{1,0:T(8,128)(2,1)} %tok.1, f32[1,8192]{1,0:T(1,128)} %bitcast.3, ...), custom_call_target="tpu_custom_call" | custom-call | tf_op jit(solution)/shard_map/gather_project/pallas_call | solution.py:344
  69.9 0.0 copy-start
  69.9 1.2 copy-done
  71.1 0.0 copy-start.1
  71.1 1.0 copy-done.1
  72.2 0.0 copy-start.2
  72.2 0.9 copy-done.2
  73.1 0.0 copy-start.3
  73.1 0.9 copy-done.3
  74.0 0.0 copy-start.4
  74.0 0.8 copy-done.4
  74.8 0.0 copy-start.5
  74.8 0.8 copy-done.5
  75.7 9.1 %attention.1.mixture = bf16[256,1024]{1,0:T(8,128)(2,1)S(1)} custom-call(bf16[256,1024]{1,0:T(8,128)(2,1)S(1)} %copy-done.1, bf16[8,2,2,128,128]{4,3,2,1,0:T(8,128)(2,1)S(1)} %copy-done, bf16[256,128]{1,0:T(8,128)(2,1)S(1)} %copy-done.4, bf16[256,128]{1,0:T(8,128)(2,1)S(1)} %copy-done.5, f32[256,128]{1,0:T(8,128)S(1)} %copy-done.2, ...), custom_call_target="tpu_custom_call" | custom-call | tf_op jit(solution)/shard_map/attention/pallas_call | solution.py:430
  84.8 0.0 copy-done.6
  84.8 47.7 %project_out.1 = bf16[3,128,1024]{2,1,0:T(8,128)(2,1)S(1)} custom-call(bf16[256,1024]{1,0:T(8,128)(2,1)S(1)} %attention.1.mixture, bf16[1024,8192]{1,0:T(8,128)(2,1)} %weight.1, s32[4]{0:T(128)S(1)} %copy-done.6), custom_call_target="tpu_custom_call" | custom-call | tf_op jit(solution)/shard_map/project_out/pallas_call | solution.py:609
  132.5 0.9 copy.16
  (1 shorter events, 0.0 us)
Async XLA Ops:
  0.0 84.8 %copy-start.6 = (s32[4]{0:T(128)S(1)}, s32[4]{0:T(128)}, u32[]{:S(2)}) copy-start(s32[4]{0:T(128)} %destination.1) | copy-start | bytes 52
  69.9 1.2 copy-start
  71.1 1.0 copy-start.1
  72.2 0.9 copy-start.2
  73.1 0.9 copy-start.3
  74.0 0.8 copy-start.4
  74.8 0.8 copy-start.5

commit v3 on v2

--- a/solution.py
+++ b/solution.py
@@ -47,7 +47,7 @@
 
 
 def project_kernel(
-    grid, seqs, tok, gain_hbm, inverse, lengths, wq, wk, wv, cached,
+    grid, seqs, greet_workers, after_weights, tok, gain_hbm, inverse, lengths, wq, wk, wv, cached,
     q_out, k_out, v_out, cosine, sine, ctx,
     xg, gain, raw, kvt, wq_all, wk_all, wv_all, qacc, kacc, vacc, squares,
     weight_sem, send_sem, recv_sem, old_send, old_recv, own_sem, load_sem,
@@ -103,6 +103,14 @@
         return carry
 
     lax.fori_loop(1, n, greet, 0)
+    workers = lax.axis_size("worker") if greet_workers else 1
+    for k in range(1, workers):
+        pl.semaphore_signal(
+            barrier,
+            inc=1,
+            device_id={"worker": lax.rem(worker + k, workers)},
+            device_id_type=MESH,
+        )
 
     def own_part(c):
         span = pl.ds(pl.multiple_of(c * part, part), part)
@@ -129,7 +137,7 @@
         return carry
 
     lax.fori_loop(1, reach, spread, 0)
-    pl.semaphore_wait(barrier, n - 1)
+    pl.semaphore_wait(barrier, n - 2 + workers)
 
     def remote(src, block, c, way, target):
         return pltpu.make_async_remote_copy(
@@ -169,6 +177,8 @@
     if columns > 1:
         start_weights(across)
         lax.fori_loop(1, reach, spread_across, 0)
+    if after_weights is not None:
+        after_weights()
 
     load_cached.wait()
     for seq in range(raw.shape[0]):
@@ -200,15 +210,10 @@
 
     own = pltpu.make_async_copy(kvt.at[lax.div(me, share)], ctx.at[me], own_sem)
     own.start()
-    each = -(-(n - 1) // reach)
-
-    def send_stored(k):
-        for extra in range(each):
-            number = 1 + k * each + extra
-
-            @pl.when(number < n)
-            def _():
-                stored(number).start()
+
+    def send_stored(k, carry):
+        stored(k).start()
+        return carry
 
     qacc[...] = jnp.zeros_like(qacc)
     kacc[...] = jnp.zeros_like(kacc)
@@ -234,7 +239,6 @@
     load_gain.wait()
     for copy in own_parts:
         copy.wait()
-    send_stored(0)
 
     def own_body(c, carry):
         multiply(me, c)
@@ -256,8 +260,6 @@
         remote(xg.at[block, c], block, c, 0, across).wait_recv()
 
     def along(k, carry):
-        send_stored(k)
-
         def piece(number, carry):
             c, side = lax.div(number, 2), lax.rem(number, 2)
             block = source(k, side, column)
@@ -274,6 +276,7 @@
         return lax.fori_loop(0, 2 * parts, piece, carry)
 
     lax.fori_loop(1, reach, along, 0)
+    lax.fori_loop(1, n, send_stored, 0)
 
     def beyond(k, carry):
         def piece(number, carry):
@@ -330,54 +333,86 @@
     own.wait()
 
 
-def project(grid, n, tokens, gain, inverse, lengths, wq, wk, wv, cached):
+def project_scratch(grid, n, tokens, gain, wq, wk, cached):
     rows, width = tokens.shape
     part = max(HD, width // 4)
     parts = width // part
+    cols, narrow = wq.shape[1], wk.shape[1]
+    ways = 2 + (grid[1] > 1)
+    return [
+        pltpu.VMEM((n, parts, rows, part), jnp.bfloat16),
+        pltpu.VMEM(gain.shape, jnp.float32),
+        pltpu.VMEM(cached.shape, jnp.bfloat16),
+        pltpu.VMEM((KVH, cached.shape[0], 2, cached.shape[1], HD), jnp.bfloat16),
+        pltpu.VMEM((n, width, cols), jnp.bfloat16),
+        pltpu.VMEM((n, width, narrow), jnp.bfloat16),
+        pltpu.VMEM((n, width, narrow), jnp.bfloat16),
+        pltpu.VMEM((rows, cols), jnp.float32),
+        pltpu.VMEM((rows, narrow), jnp.float32),
+        pltpu.VMEM((rows, narrow), jnp.float32),
+        pltpu.VMEM((rows, 1), jnp.float32),
+        pltpu.SemaphoreType.DMA((n, 3)),
+        pltpu.SemaphoreType.DMA((ways, n, parts)),
+        pltpu.SemaphoreType.DMA((n, parts)),
+        pltpu.SemaphoreType.DMA((n,)),
+        pltpu.SemaphoreType.DMA((n,)),
+        pltpu.SemaphoreType.DMA,
+        pltpu.SemaphoreType.DMA((parts + 2,)),
+    ]
+
+
+def project(grid, n, tokens, gain, inverse, lengths, wq, wk, wv, cached):
+    rows = tokens.shape[0]
     cols, narrow = wq.shape[1], wk.shape[1]
     seqs, stored = cached.shape[0], cached.shape[1]
     vmem = pl.BlockSpec(memory_space=pltpu.VMEM)
     smem = pl.BlockSpec(memory_space=pltpu.SMEM)
     anywhere = pl.BlockSpec(memory_space=pl.ANY)
-    kvt = (KVH, seqs, 2, stored, HD)
-    ways = 2 + (grid[1] > 1)
     return pl.pallas_call(
-        functools.partial(project_kernel, grid, seqs),
+        functools.partial(project_kernel, grid, seqs, False, None),
         out_shape=(
             jax.ShapeDtypeStruct((rows, cols), jnp.bfloat16),
             jax.ShapeDtypeStruct((rows, narrow), jnp.bfloat16),
             jax.ShapeDtypeStruct((rows, narrow), jnp.bfloat16),
             jax.ShapeDtypeStruct((rows, HD), jnp.float32),
             jax.ShapeDtypeStruct((rows, HD), jnp.float32),
-            jax.ShapeDtypeStruct((n,) + kvt[1:], jnp.bfloat16),
+            jax.ShapeDtypeStruct((n, seqs, 2, stored, HD), jnp.bfloat16),
         ),
         in_specs=[anywhere, anywhere, vmem, smem] + [anywhere] * 4,
         out_specs=(vmem,) * 5 + (anywhere,),
-        scratch_shapes=[
-            pltpu.VMEM((n, parts, rows, part), jnp.bfloat16),
-            pltpu.VMEM(gain.shape, jnp.float32),
-            pltpu.VMEM(cached.shape, jnp.bfloat16),
-            pltpu.VMEM(kvt, jnp.bfloat16),
-            pltpu.VMEM((n, width, cols), jnp.bfloat16),
-            pltpu.VMEM((n, width, narrow), jnp.bfloat16),
-            pltpu.VMEM((n, width, narrow), jnp.bfloat16),
-            pltpu.VMEM((rows, cols), jnp.float32),
-            pltpu.VMEM((rows, narrow), jnp.float32),
-            pltpu.VMEM((rows, narrow), jnp.float32),
-            pltpu.VMEM((rows, 1), jnp.float32),
-            pltpu.SemaphoreType.DMA((n, 3)),
-            pltpu.SemaphoreType.DMA((ways, n, parts)),
-            pltpu.SemaphoreType.DMA((n, parts)),
-            pltpu.SemaphoreType.DMA((n,)),
-            pltpu.SemaphoreType.DMA((n,)),
-            pltpu.SemaphoreType.DMA,
-            pltpu.SemaphoreType.DMA((parts + 2,)),
-        ],
+        scratch_shapes=project_scratch(grid, n, tokens, gain, wq, wk, cached),
         compiler_params=pltpu.CompilerParams(
             collective_id=0, has_side_effects=True, vmem_limit_bytes=60 * 2**20
         ),
         name="gather_project",
     )(tokens, gain, inverse, lengths, wq, wk, wv, cached)
+
+
+def attend_heads(query, old_key, old_value, key, value, seen, mixture, heads, lines):
+    scale = math.log2(math.e) / math.sqrt(HD)
+    contract = (((1,), (1,)), ((), ()))
+    row = lax.broadcasted_iota(jnp.int32, (NEW, NEW), 0)
+    col = lax.broadcasted_iota(jnp.int32, (NEW, NEW), 1)
+    for cols in heads:
+        one = query[lines, cols]
+        old_scores = lax.dot_general(one, old_key, contract, preferred_element_type=jnp.float32)
+        new_scores = lax.dot_general(one, key, contract, preferred_element_type=jnp.float32)
+        old_scores = jnp.where(seen, old_scores * scale, -1e30)
+        new_scores = jnp.where(row >= col, new_scores * scale, -1e30)
+        largest = jnp.maximum(
+            jnp.max(old_scores, axis=1, keepdims=True),
+            jnp.max(new_scores, axis=1, keepdims=True),
+        )
+        old_expo = jnp.exp2(old_scores - largest)
+        new_expo = jnp.exp2(new_scores - largest)
+        inverse = 1.0 / (
+            jnp.sum(old_expo, axis=1, keepdims=True) + jnp.sum(new_expo, axis=1, keepdims=True)
+        )
+        old_probs = (old_expo * inverse).astype(jnp.bfloat16)
+        new_probs = (new_expo * inverse).astype(jnp.bfloat16)
+        mixed = jnp.dot(old_probs, old_value, preferred_element_type=jnp.float32)
+        mixed += jnp.dot(new_probs, value, preferred_element_type=jnp.float32)
+        mixture[lines, cols] = mixed.astype(jnp.bfloat16)
 
 
 def attend_kernel(query, old, key_raw, value, cosine, sine, bias, mixture, key_turned):
@@ -387,38 +422,18 @@
         turned = pltpu.roll(raw, HD // 2, 1)
         key_turned[...] = (raw * cosine[...] + turned * sine[...]).astype(jnp.bfloat16)
 
-    heads = query.shape[1] // HD
     count = old.shape[0] * old.shape[3]
-    old_key = old[:, 0, 0].reshape(count, HD)
-    old_value = old[:, 0, 1].reshape(count, HD)
-    scale = math.log2(math.e) / math.sqrt(HD)
-    contract = (((1,), (1,)), ((), ()))
-    seen = bias[0] > 0
-    row = lax.broadcasted_iota(jnp.int32, (NEW, NEW), 0)
-    col = lax.broadcasted_iota(jnp.int32, (NEW, NEW), 1)
-    for head in range(heads):
-        cols = slice(head * HD, (head + 1) * HD)
-        one = query[:, cols]
-        old_scores = lax.dot_general(one, old_key, contract, preferred_element_type=jnp.float32)
-        new_scores = lax.dot_general(
-            one, key_turned[...], contract, preferred_element_type=jnp.float32
-        )
-        old_scores = jnp.where(seen, old_scores * scale, -1e30)
-        new_scores = jnp.where(row >= col, new_scores * scale, -1e30)
-        largest = jnp.maximum(
-            jnp.max(old_scores, axis=1, keepdims=True),
-            jnp.max(new_scores, axis=1, keepdims=True),
-        )
-        old_expo = jnp.exp2(old_scores - largest)
-        new_expo = jnp.exp2(new_scores - largest)
-        inverse = 1.0 / (
-            jnp.sum(old_expo, axis=1, keepdims=True) + jnp.sum(new_expo, axis=1, keepdims=True)
-        )
-        old_probs = (old_expo * inverse).astype(jnp.bfloat16)
-        new_probs = (new_expo * inverse).astype(jnp.bfloat16)
-        mixed = jnp.dot(old_probs, old_value, preferred_element_type=jnp.float32)
-        mixed += jnp.dot(new_probs, value[...], preferred_element_type=jnp.float32)
-        mixture[:, cols] = mixed.astype(jnp.bfloat16)
+    attend_heads(
+        query,
+        old[:, 0, 0].reshape(count, HD),
+        old[:, 0, 1].reshape(count, HD),
+        key_turned[...],
+        value[...],
+        bias[0] > 0,
+        mixture,
+        [slice(head * HD, (head + 1) * HD) for head in range(query.shape[1] // HD)],
+        slice(None),
+    )
 
 
 def attention(query, old, key_raw, value, cosine, sine, bias):
@@ -447,8 +462,8 @@
     )(query, old, key_raw, value, cosine, sine, bias)
 
 
-def output_kernel(
-    order, mixture, weight, destination, result,
+def output_phases(
+    order, greet, mixture, weight, destination, result,
     everyone, weight_all, outgoing, incoming,
     weight_sem, send_sem, recv_sem, swap_send, swap_recv,
 ):
@@ -463,18 +478,6 @@
     forward = index(lax.rem(place + 1, n))
     back = index(lax.rem(place + n - 1, n))
     targets = (forward, back)
-    streams = [(d, c) for c in range(2) for d in range(2)]
-
-    barrier = pltpu.get_barrier_semaphore()
-    for target in targets:
-        pl.semaphore_signal(barrier, inc=1, device_id={"tensor": target}, device_id_type=MESH)
-    for k in range(1, workers):
-        pl.semaphore_signal(
-            barrier,
-            inc=1,
-            device_id={"worker": lax.rem(worker + k, workers)},
-            device_id_type=MESH,
-        )
 
     def weight_copy(block):
         cols = pl.ds(pl.multiple_of(block * width, width), width)
@@ -491,120 +494,173 @@
 
         return carry
 
-    lax.fori_loop(0, n // 2, start_weights, 0)
-    weight_copy(me).start()
-    for d, c in streams:
-        incoming[0, d, c] = jnp.zeros((half, part), jnp.bfloat16)
-    pl.semaphore_wait(barrier, 1 + workers)
-
-    def hop(step, d, c):
+    def begin():
+        if greet:
+            barrier = pltpu.get_barrier_semaphore()
+            for target in targets:
+                pl.semaphore_signal(
+                    barrier, inc=1, device_id={"tensor": target}, device_id_type=MESH
+                )
+            for k in range(1, workers):
+                pl.semaphore_signal(
+                    barrier,
+                    inc=1,
+                    device_id={"worker": lax.rem(worker + k, workers)},
+                    device_id_type=MESH,
+                )
+        lax.fori_loop(0, n // 2, start_weights, 0)
+        weight_copy(me).start()
+        for r in range(2):
+            for d in range(2):
+                incoming[0, r, d] = jnp.zeros((half, part), jnp.bfloat16)
+        if greet:
+            pl.semaphore_wait(barrier, 1 + workers)
+
+    def hop(step, r, d):
         return pltpu.make_async_remote_copy(
-            src_ref=outgoing.at[step, d, c],
-            dst_ref=incoming.at[step + 1, d, c],
-            send_sem=send_sem.at[step, d, c],
-            recv_sem=recv_sem.at[step + 1, d, c],
+            src_ref=outgoing.at[step, r, d],
+            dst_ref=incoming.at[step + 1, r, d],
+            send_sem=send_sem.at[step, r, d],
+            recv_sem=recv_sem.at[step + 1, r, d],
             device_id={"tensor": targets[d]},
             device_id_type=MESH,
         )
 
-    def arrival(step, d, c):
+    def arrival(step, r, d):
         return pltpu.make_async_remote_copy(
-            src_ref=outgoing.at[step, d, c],
-            dst_ref=incoming.at[step, d, c],
-            send_sem=send_sem.at[step, d, c],
-            recv_sem=recv_sem.at[step, d, c],
+            src_ref=outgoing.at[step, r, d],
+            dst_ref=incoming.at[step, r, d],
+            send_sem=send_sem.at[step, r, d],
+            recv_sem=recv_sem.at[step, r, d],
             device_id={"tensor": targets[d]},
             device_id_type=MESH,
         )
 
-    def step_body(step, carry):
+    def add_up(step, r):
         blocks = (
             index(lax.rem(place + 2 * n - 1 - step, n)),
             index(lax.rem(place + 1 + step, n)),
         )
 
-        @pl.when(step < n // 2)
-        def _():
-            weight_copy(blocks[0]).wait()
-
-        @pl.when(step < n // 2 - 1)
-        def _():
-            weight_copy(blocks[1]).wait()
-
-        @pl.when(step == n // 2)
-        def _():
-            weight_copy(me).wait()
-
-        for d, c in streams:
+        if r == 0:
+
+            @pl.when(step < n // 2)
+            def _():
+                weight_copy(blocks[0]).wait()
+
+            @pl.when(step < n // 2 - 1)
+            def _():
+                weight_copy(blocks[1]).wait()
+
+            @pl.when(step == n // 2)
+            def _():
+                weight_copy(me).wait()
+
+        for d in range(2):
             product = jnp.dot(
-                mixture[d * half : (d + 1) * half, :],
-                weight_all[blocks[d], :, c * part : (c + 1) * part],
+                mixture[r * half : (r + 1) * half, :],
+                weight_all[blocks[d], :, d * part : (d + 1) * part],
                 preferred_element_type=jnp.float32,
             )
 
             @pl.when(step > 0)
             def _():
-                arrival(step, d, c).wait_recv()
-
-            summed = product + incoming[step, d, c].astype(jnp.float32)
-            outgoing[step, d, c] = summed.astype(jnp.bfloat16)
+                arrival(step, r, d).wait_recv()
+
+            summed = product + incoming[step, r, d].astype(jnp.float32)
+            outgoing[step, r, d] = summed.astype(jnp.bfloat16)
 
             @pl.when(step < n - 1)
             def _():
-                hop(step, d, c).start()
-
-        return carry
-
-    lax.fori_loop(0, n, step_body, 0)
-
-    swaps = []
-    for d in range(2):
-        lines = slice(d * half, (d + 1) * half)
-        for c in range(2):
-            everyone[worker, lines, c * part : (c + 1) * part] = outgoing[n - 1, d, c]
+                hop(step, r, d).start()
+
+    def swap(k, r):
+        return pltpu.make_async_remote_copy(
+            src_ref=everyone.at[worker, pl.ds(r * half, half)],
+            dst_ref=everyone.at[worker, pl.ds(r * half, half)],
+            send_sem=swap_send.at[k, r],
+            recv_sem=swap_recv.at[k, r],
+            device_id={"worker": lax.rem(worker + k, workers)},
+            device_id_type=MESH,
+        )
+
+    def hand_over(r):
+        for d in range(2):
+            everyone[worker, r * half : (r + 1) * half, d * part : (d + 1) * part] = outgoing[
+                n - 1, r, d
+            ]
         for k in range(1, workers):
-            swap = pltpu.make_async_remote_copy(
-                src_ref=everyone.at[worker, pl.ds(d * half, half)],
-                dst_ref=everyone.at[worker, pl.ds(d * half, half)],
-                send_sem=swap_send.at[k, d],
-                recv_sem=swap_recv.at[k, d],
-                device_id={"worker": lax.rem(worker + k, workers)},
-                device_id_type=MESH,
-            )
-            swap.start()
-            swaps.append(swap)
-
-    def finish(step, carry):
-        for d, c in streams:
-            hop(step, d, c).wait_send()
-        return carry
-
-    lax.fori_loop(0, n - 1, finish, 0)
-    for swap in swaps:
-        swap.wait()
-
-    seqs = destination.shape[0]
-    local_seqs = seqs // workers
-    bound = [jnp.where(destination[seq] == worker, 1, 0) for seq in range(seqs)]
-    rank, ranks = 0, []
-    for seq in range(seqs):
-        ranks.append(rank)
-        rank = rank + bound[seq]
-    for slot in range(result.shape[0]):
-        chosen = [jnp.where(ranks[seq] == slot, bound[seq], 0) for seq in range(seqs)]
-        picked = jnp.zeros(result.shape[1:], result.dtype)
+            swap(k, r).start()
+
+    def sums():
+        def step_body(step, carry):
+            add_up(step + 1, 0)
+            add_up(step, 1)
+            return carry
+
+        lax.fori_loop(0, n - 1, step_body, 0)
+        hand_over(0)
+        add_up(n - 1, 1)
+        hand_over(1)
+
+    def end():
+        def finish(step, carry):
+            for r in range(2):
+                for d in range(2):
+                    hop(step, r, d).wait_send()
+            return carry
+
+        lax.fori_loop(0, n - 1, finish, 0)
+        for r in range(2):
+            for k in range(1, workers):
+                swap(k, r).wait()
+
+        seqs = destination.shape[0]
+        local_seqs = seqs // workers
+        bound = [jnp.where(destination[seq] == worker, 1, 0) for seq in range(seqs)]
+        rank, ranks = 0, []
         for seq in range(seqs):
-            first = seq % local_seqs * NEW
-            rows = everyone[seq // local_seqs, first : first + NEW, :]
-            flag = jnp.full(result.shape[1:], chosen[seq], jnp.int32)
-            picked = jnp.where(flag > 0, rows, picked)
-        result[slot] = picked
+            ranks.append(rank)
+            rank = rank + bound[seq]
+        for slot in range(result.shape[0]):
+            chosen = [jnp.where(ranks[seq] == slot, bound[seq], 0) for seq in range(seqs)]
+            picked = jnp.zeros(result.shape[1:], result.dtype)
+            for seq in range(seqs):
+                first = seq % local_seqs * NEW
+                rows = everyone[seq // local_seqs, first : first + NEW, :]
+                flag = jnp.full(result.shape[1:], chosen[seq], jnp.int32)
+                picked = jnp.where(flag > 0, rows, picked)
+            result[slot] = picked
+
+    return begin, add_up, sums, end
+
+
+def output_kernel(order, *refs):
+    begin, add_up, sums, end = output_phases(order, True, *refs)
+    begin()
+    add_up(0, 0)
+    sums()
+    end()
+
+
+def output_scratch(n, workers, rows, depth, width):
+    half, part = rows // 2, width // 2
+    return [
+        pltpu.VMEM((workers, rows, width), jnp.bfloat16),
+        pltpu.VMEM((n, depth, width), jnp.bfloat16),
+        pltpu.VMEM((n, 2, 2, half, part), jnp.bfloat16),
+        pltpu.VMEM((n, 2, 2, half, part), jnp.bfloat16),
+        pltpu.SemaphoreType.DMA((n,)),
+        pltpu.SemaphoreType.DMA((n, 2, 2)),
+        pltpu.SemaphoreType.DMA((n, 2, 2)),
+        pltpu.SemaphoreType.DMA((workers, 2)),
+        pltpu.SemaphoreType.DMA((workers, 2)),
+    ]
 
 
 def project_out(order, n, workers, mixture, weight, destination):
     rows, depth = mixture.shape
     width = weight.shape[1] // n
-    half, part = rows // 2, width // 2
     vmem = pl.BlockSpec(memory_space=pltpu.VMEM)
     return pl.pallas_call(
         functools.partial(output_kernel, order),
@@ -615,22 +671,97 @@
             pl.BlockSpec(memory_space=pltpu.SMEM),
         ],
         out_specs=vmem,
-        scratch_shapes=[
-            pltpu.VMEM((workers, rows, width), jnp.bfloat16),
-            pltpu.VMEM((n, depth, width), jnp.bfloat16),
-            pltpu.VMEM((n, 2, 2, half, part), jnp.bfloat16),
-            pltpu.VMEM((n, 2, 2, half, part), jnp.bfloat16),
-            pltpu.SemaphoreType.DMA((n,)),
-            pltpu.SemaphoreType.DMA((n, 2, 2)),
-            pltpu.SemaphoreType.DMA((n, 2, 2)),
-            pltpu.SemaphoreType.DMA((workers, 2)),
-            pltpu.SemaphoreType.DMA((workers, 2)),
-        ],
+        scratch_shapes=output_scratch(n, workers, rows, depth, width),
         compiler_params=pltpu.CompilerParams(
             collective_id=1, has_side_effects=True, vmem_limit_bytes=48 * 2**20
         ),
         name="project_out",
     )(mixture, weight, destination)
+
+
+def layer_kernel(
+    order, grid, seqs, scratch_counts,
+    tok, gain, inverse, lengths, wq, wk, wv, cached, bias, weight, destination, result,
+    query, key_raw, value, cosine, sine, ctx, mixture, *scratch,
+):
+    first = scratch_counts
+    begin, add_up, sums, end = output_phases(
+        order, False, mixture, weight, destination, result, *scratch[first:]
+    )
+    project_kernel(
+        grid, seqs, True, begin, tok, gain, inverse, lengths, wq, wk, wv, cached,
+        query, key_raw, value, cosine, sine, ctx, *scratch[:first],
+    )
+    worker = lax.axis_index("worker")
+    count = ctx.shape[0] * ctx.shape[3]
+    heads = query.shape[1] // HD
+    together = math.gcd(heads, 4)
+
+    def attend(seq):
+        lines = slice(seq * NEW, (seq + 1) * NEW)
+        raw = key_raw[lines, :].astype(jnp.float32)
+        turned = pltpu.roll(raw, HD // 2, 1)
+        key = (raw * cosine[lines, :] + turned * sine[lines, :]).astype(jnp.bfloat16)
+        key_raw[lines, :] = key
+
+        def some(number, carry):
+            attend_heads(
+                query,
+                ctx[:, seq, 0].reshape(count, HD),
+                ctx[:, seq, 1].reshape(count, HD),
+                key_raw[lines, :],
+                value[lines, :],
+                bias[worker * seqs + seq] > 0,
+                mixture,
+                [
+                    pl.ds(pl.multiple_of((number * together + k) * HD, HD), HD)
+                    for k in range(together)
+                ],
+                lines,
+            )
+            return carry
+
+        lax.fori_loop(0, heads // together, some, 0)
+
+    for seq in range(seqs // 2):
+        attend(seq)
+    add_up(0, 0)
+    for seq in range(seqs // 2, seqs):
+        attend(seq)
+    sums()
+    end()
+
+
+def layer(order, grid, n, workers, tokens, gain, inverse, lengths, wq, wk, wv, cached, bias, weight, destination):
+    rows = tokens.shape[0]
+    cols, narrow = wq.shape[1], wk.shape[1]
+    width = weight.shape[1] // n
+    seqs, stored = cached.shape[0], cached.shape[1]
+    vmem = pl.BlockSpec(memory_space=pltpu.VMEM)
+    smem = pl.BlockSpec(memory_space=pltpu.SMEM)
+    anywhere = pl.BlockSpec(memory_space=pl.ANY)
+    scratch = project_scratch(grid, n, tokens, gain, wq, wk, cached)
+    return pl.pallas_call(
+        functools.partial(layer_kernel, order, grid, seqs, len(scratch)),
+        out_shape=jax.ShapeDtypeStruct((CAP, NEW, width), jnp.bfloat16),
+        in_specs=[anywhere, anywhere, vmem, smem] + [anywhere] * 4 + [vmem, anywhere, smem],
+        out_specs=vmem,
+        scratch_shapes=[
+            pltpu.VMEM((rows, cols), jnp.bfloat16),
+            pltpu.VMEM((rows, narrow), jnp.bfloat16),
+            pltpu.VMEM((rows, narrow), jnp.bfloat16),
+            pltpu.VMEM((rows, HD), jnp.float32),
+            pltpu.VMEM((rows, HD), jnp.float32),
+            pltpu.VMEM((n, seqs, 2, stored, HD), jnp.bfloat16),
+            pltpu.VMEM((rows, cols), jnp.bfloat16),
+        ]
+        + scratch
+        + output_scratch(n, workers, rows, cols, width),
+        compiler_params=pltpu.CompilerParams(
+            collective_id=2, has_side_effects=True, vmem_limit_bytes=62 * 2**20
+        ),
+        name="layer",
+    )(tokens, gain, inverse, lengths, wq, wk, wv, cached, bias, weight, destination)
 
 
 def from_partner(block, axis, bit):
@@ -673,20 +804,25 @@
     n = lax.axis_size("tensor")
     workers = lax.axis_size("worker")
     seqs = cached_blocks.shape[0]
-    first = lax.axis_index("worker") * seqs
-    lengths = lax.dynamic_slice_in_dim(cache_length, first, seqs, 0)
-    tables = lax.dynamic_slice_in_dim(block_table, first, seqs, 0)
-    logical = tables[:, :, None] * BLK + jnp.arange(BLK, dtype=jnp.int32)[None, None, :]
-    seen = (logical < lengths[:, None, None]).astype(jnp.float32).reshape(seqs, 1, -1)
-
+    logical = block_table[:, :, None] * BLK + jnp.arange(BLK, dtype=jnp.int32)[None, None, :]
+    seen = (logical < cache_length[:, None, None]).astype(jnp.float32)
+    seen = seen.reshape(cache_length.shape[0], 1, -1)
     half = 500000.0 ** (-(np.arange(HD // 2) * 2.0 / HD))
     inverse = jnp.asarray(np.concatenate([half, half])[None, :], jnp.float32)
+    gain = norm_gain[None, :]
+    bits = (n // KVH).bit_length() - 1
+    if bits == 0:
+        return layer(
+            ring, grid, n, workers, tokens, gain, inverse, cache_length,
+            query_weight, key_weight, value_weight, cached_blocks, seen,
+            output_weight, destination,
+        )[None]
     query, key_raw, value, cosine, sine, old = project(
-        grid, n, tokens, norm_gain[None, :], inverse, cache_length,
+        grid, n, tokens, gain, inverse, cache_length,
         query_weight, key_weight, value_weight, cached_blocks,
     )
-    bits = (n // KVH).bit_length() - 1
     key_raw, value = whole_head(key_raw, bits), whole_head(value, bits)
+    seen = lax.dynamic_slice_in_dim(seen, lax.axis_index("worker") * seqs, seqs, 0)
     mixture = attention(query, old, key_raw, value, cosine, sine, seen)
     return project_out(ring, n, workers, mixture, output_weight, destination)[None]
 

time: 134 us -> 126 us (0.940)
  local copies, waits for them, and re-layouts: 7.63 us -> 2.35 us
  Pallas kernels: 125 us -> 121 us
    unnamed x15 -> x1, local copies, waits for them, and re-layouts: 6.63 us -> 2.06 us
    pallas_call x3 -> x1, Pallas kernels: 125 us -> 121 us  [layer(): pl.pallas_call(functools.partial(layer_kernel, order, grid, seqs, len(scr...]
where the time goes in v3:
time: 126 us
  Pallas kernels  121 us (96%)
  local copies, waits for them, and re-layouts  2.35 us (2%)
  other arithmetic  2.02 us (2%)
    pallas_call x1, Pallas kernels, layer(): pl.pallas_call(functools.partial(layer_kernel, order, grid, seqs, len(scr...  121 us

profile of v3, /device:TPU:0, one launch (start us, length us, event | category | flops | bytes accessed | tf_op | source)
XLA Modules:
  0.0 125.6 jit_solution(8511568356138840842)
XLA Ops:
  0.0 0.7 broadcast_multiply_fusion
  0.7 0.1 add.29
  0.8 0.1 add.26
  0.9 0.1 add.32
  1.0 1.3 %compare_convert_fusion.bias = f32[4,1,1024]{2,1,0:T(1,128)} fusion(s32[4,1,1024]{2,1,0:T(1,128)S(1)} %add.32, s32[4]{0:T(128)} %lengths.1, s32[1024]{0:T(1024)S(1)} %add.29), kind=kLoop, calls=%fused_computation | loop fusion | flops 12288 | bytes 36880 | tf_op jit(solution)/shard_map/convert_element_type | solution.py:808
  2.3 121.2 %layer.1 = bf16[3,128,1024]{2,1,0:T(8,128)(2,1)} custom-call(bf16[256,1024]{1,0:T(8,128)(2,1)} %tok.1, f32[1,8192]{1,0:T(1,128)} %bitcast.3, f32[1,128]{1,0:T(1,128)} %constant.4.clone.inverse, s32[4]{0:T(128)} %lengths.1, bf16[8192,1024]{1,0:T(8,128)(2,1)} %wq.1, bf16[8192,128]{1,0:T(8,128)(2,1)} %wk.1, bf16[8192,128]{1,0:T(8,128)(2,1)} %wv.1, ...), custom_call_target="tpu_custom_call" | custom-call | tf_op jit(solution)/shard_map/layer/pallas_call | solution.py:744
  123.5 2.1 %copy.16 = bf16[1,3,128,1024]{3,2,1,0:T(8,128)(2,1)} copy(bf16[1,3,128,1024]{3,2,1,0:T(8,128)(2,1)} %bitcast.2) | data formatting | bytes 1572864
  (1 shorter events, 0.0 us)

commit v4 on v3

--- a/solution.py
+++ b/solution.py
@@ -180,11 +180,16 @@
     if after_weights is not None:
         after_weights()
 
-    load_cached.wait()
-    for seq in range(raw.shape[0]):
-        for kind in range(2):
-            for head in range(kvt.shape[0]):
-                kvt[head, seq, kind] = raw[seq, :, kind, head * HD : (head + 1) * HD]
+    units = kvt.shape[0] * raw.shape[0]
+    per_piece = -(-units // (2 * parts * (reach - 1)))
+
+    def reorder(unit):
+        @pl.when(unit < units)
+        def _():
+            head, seq = lax.div(unit, raw.shape[0]), lax.rem(unit, raw.shape[0])
+            span = pl.ds(pl.multiple_of(head * HD, HD), HD)
+            for kind in range(2):
+                kvt[head, seq, kind] = raw[seq, :, kind, span]
 
     def stored(k):
         target = lax.rem(me + k, n)
@@ -208,9 +213,6 @@
             device_id_type=MESH,
         )
 
-    own = pltpu.make_async_copy(kvt.at[lax.div(me, share)], ctx.at[me], own_sem)
-    own.start()
-
     def send_stored(k, carry):
         stored(k).start()
         return carry
@@ -237,6 +239,7 @@
             )
 
     load_gain.wait()
+    load_cached.wait()
     for copy in own_parts:
         copy.wait()
 
@@ -245,6 +248,32 @@
         return carry
 
     lax.fori_loop(0, parts, own_body, 0)
+
+    def arrive(block, c):
+        remote(xg.at[block, c], block, c, 0, across).wait_recv()
+
+    def along(k, carry):
+        def piece(number, carry):
+            c, side = lax.div(number, 2), lax.rem(number, 2)
+            block = source(k, side, column)
+
+            @pl.when(comes(k, side))
+            def _():
+                arrive(block, c)
+                for needed, copy in onward(k, side, block, c):
+                    pl.when(needed)(copy.start)
+                multiply(block, c)
+
+            for extra in range(per_piece):
+                reorder(((k - 1) * 2 * parts + number) * per_piece + extra)
+            return carry
+
+        return lax.fori_loop(0, 2 * parts, piece, carry)
+
+    lax.fori_loop(1, reach, along, 0)
+    lax.fori_loop(1, n, send_stored, 0)
+    own = pltpu.make_async_copy(kvt.at[lax.div(me, share)], ctx.at[me], own_sem)
+    own.start()
 
     for seq in range(seqs):
         span = slice(seq * NEW, (seq + 1) * NEW)
@@ -255,28 +284,6 @@
         cosine[span, :] = jnp.cos(angle)
         turn = jnp.sin(angle)
         sine[span, :] = jnp.where(lane < HD // 2, -turn, turn)
-
-    def arrive(block, c):
-        remote(xg.at[block, c], block, c, 0, across).wait_recv()
-
-    def along(k, carry):
-        def piece(number, carry):
-            c, side = lax.div(number, 2), lax.rem(number, 2)
-            block = source(k, side, column)
-
-            @pl.when(comes(k, side))
-            def _():
-                arrive(block, c)
-                for needed, copy in onward(k, side, block, c):
-                    pl.when(needed)(copy.start)
-                multiply(block, c)
-
-            return carry
-
-        return lax.fori_loop(0, 2 * parts, piece, carry)
-
-    lax.fori_loop(1, reach, along, 0)
-    lax.fori_loop(1, n, send_stored, 0)
 
     def beyond(k, carry):
         def piece(number, carry):
@@ -464,7 +471,7 @@
 
 def output_phases(
     order, greet, mixture, weight, destination, result,
-    everyone, weight_all, outgoing, incoming,
+    everyone, weight_all, incoming,
     weight_sem, send_sem, recv_sem, swap_send, swap_recv,
 ):
     position, index = order
@@ -518,7 +525,7 @@
 
     def hop(step, r, d):
         return pltpu.make_async_remote_copy(
-            src_ref=outgoing.at[step, r, d],
+            src_ref=incoming.at[step, r, d],
             dst_ref=incoming.at[step + 1, r, d],
             send_sem=send_sem.at[step, r, d],
             recv_sem=recv_sem.at[step + 1, r, d],
@@ -528,7 +535,7 @@
 
     def arrival(step, r, d):
         return pltpu.make_async_remote_copy(
-            src_ref=outgoing.at[step, r, d],
+            src_ref=incoming.at[step, r, d],
             dst_ref=incoming.at[step, r, d],
             send_sem=send_sem.at[step, r, d],
             recv_sem=recv_sem.at[step, r, d],
@@ -568,7 +575,7 @@
                 arrival(step, r, d).wait_recv()
 
             summed = product + incoming[step, r, d].astype(jnp.float32)
-            outgoing[step, r, d] = summed.astype(jnp.bfloat16)
+            incoming[step, r, d] = summed.astype(jnp.bfloat16)
 
             @pl.when(step < n - 1)
             def _():
@@ -586,7 +593,7 @@
 
     def hand_over(r):
         for d in range(2):
-            everyone[worker, r * half : (r + 1) * half, d * part : (d + 1) * part] = outgoing[
+            everyone[worker, r * half : (r + 1) * half, d * part : (d + 1) * part] = incoming[
                 n - 1, r, d
             ]
         for k in range(1, workers):
@@ -648,7 +655,6 @@
     return [
         pltpu.VMEM((workers, rows, width), jnp.bfloat16),
         pltpu.VMEM((n, depth, width), jnp.bfloat16),
-        pltpu.VMEM((n, 2, 2, half, part), jnp.bfloat16),
         pltpu.VMEM((n, 2, 2, half, part), jnp.bfloat16),
         pltpu.SemaphoreType.DMA((n,)),
         pltpu.SemaphoreType.DMA((n, 2, 2)),
@@ -681,8 +687,8 @@
 
 def layer_kernel(
     order, grid, seqs, scratch_counts,
-    tok, gain, inverse, lengths, wq, wk, wv, cached, bias, weight, destination, result,
-    query, key_raw, value, cosine, sine, ctx, mixture, *scratch,
+    tok, gain, inverse, lengths, wq, wk, wv, cached, tables, weight, destination, result,
+    seen, query, key_raw, value, cosine, sine, ctx, mixture, *scratch,
 ):
     first = scratch_counts
     begin, add_up, sums, end = output_phases(
@@ -697,7 +703,19 @@
     heads = query.shape[1] // HD
     together = math.gcd(heads, 4)
 
+    def look(seq):
+        row = tables[pl.ds(worker * seqs + seq, 1), :].astype(jnp.float32)
+        rows = jnp.broadcast_to(row, (8, row.shape[1])).astype(jnp.bfloat16)
+        slot = lax.broadcasted_iota(jnp.int32, (row.shape[1], count), 1)
+        block = lax.broadcasted_iota(jnp.int32, (row.shape[1], count), 0)
+        pick = jnp.where(lax.div(slot, BLK) == block, 1.0, 0.0).astype(jnp.bfloat16)
+        held = jnp.dot(rows, pick, preferred_element_type=jnp.float32)
+        inside = lax.broadcasted_iota(jnp.int32, held.shape, 1)
+        logical = held.astype(jnp.int32) * BLK + lax.rem(inside, BLK)
+        return jnp.where(logical < lengths[worker * seqs + seq], 1.0, 0.0)
+
     def attend(seq):
+        seen[...] = look(seq)
         lines = slice(seq * NEW, (seq + 1) * NEW)
         raw = key_raw[lines, :].astype(jnp.float32)
         turned = pltpu.roll(raw, HD // 2, 1)
@@ -711,7 +729,7 @@
                 ctx[:, seq, 1].reshape(count, HD),
                 key_raw[lines, :],
                 value[lines, :],
-                bias[worker * seqs + seq] > 0,
+                seen[0:1, :] > 0,
                 mixture,
                 [
                     pl.ds(pl.multiple_of((number * together + k) * HD, HD), HD)
@@ -732,7 +750,7 @@
     end()
 
 
-def layer(order, grid, n, workers, tokens, gain, inverse, lengths, wq, wk, wv, cached, bias, weight, destination):
+def layer(order, grid, n, workers, tokens, gain, inverse, lengths, wq, wk, wv, cached, tables, weight, destination):
     rows = tokens.shape[0]
     cols, narrow = wq.shape[1], wk.shape[1]
     width = weight.shape[1] // n
@@ -747,6 +765,7 @@
         in_specs=[anywhere, anywhere, vmem, smem] + [anywhere] * 4 + [vmem, anywhere, smem],
         out_specs=vmem,
         scratch_shapes=[
+            pltpu.VMEM((8, n * stored), jnp.float32),
             pltpu.VMEM((rows, cols), jnp.bfloat16),
             pltpu.VMEM((rows, narrow), jnp.bfloat16),
             pltpu.VMEM((rows, narrow), jnp.bfloat16),
@@ -758,10 +777,10 @@
         + scratch
         + output_scratch(n, workers, rows, cols, width),
         compiler_params=pltpu.CompilerParams(
-            collective_id=2, has_side_effects=True, vmem_limit_bytes=62 * 2**20
+            collective_id=2, has_side_effects=True, vmem_limit_bytes=57 * 2**20
         ),
         name="layer",
-    )(tokens, gain, inverse, lengths, wq, wk, wv, cached, bias, weight, destination)
+    )(tokens, gain, inverse, lengths, wq, wk, wv, cached, tables, weight, destination)
 
 
 def from_partner(block, axis, bit):
@@ -814,7 +833,7 @@
     if bits == 0:
         return layer(
             ring, grid, n, workers, tokens, gain, inverse, cache_length,
-            query_weight, key_weight, value_weight, cached_blocks, seen,
+            query_weight, key_weight, value_weight, cached_blocks, block_table,
             output_weight, destination,
         )[None]
     query, key_raw, value, cosine, sine, old = project(

time: 126 us -> 124 us (0.984)
  other arithmetic: 2.02 us -> 0 us
    convert_element_type x1 -> x0, other arithmetic: 1.34 us -> none  [local(): seen = (logical < cache_length[:, None, None]).astype(jnp.float32)]
where the time goes in v4:
time: 124 us; the launch traced here: 123 us
  Pallas kernels  121 us (98%)
  local copies, waits for them, and re-layouts  2.06 us (2%)
    pallas_call x1, Pallas kernels, layer(): pl.pallas_call(functools.partial(layer_kernel, order, grid, seqs, len(scr...  121 us

profile of v4, /device:TPU:0, one launch (start us, length us, event | category | flops | bytes accessed | tf_op | source)
XLA Modules:
  0.0 123.4 jit_solution(6191986556836425570)
XLA Ops:
  0.0 121.3 %layer.1 = bf16[3,128,1024]{2,1,0:T(8,128)(2,1)} custom-call(bf16[256,1024]{1,0:T(8,128)(2,1)} %tok.1, f32[1,8192]{1,0:T(1,128)} %bitcast.3, f32[1,128]{1,0:T(1,128)} %constant.2.clone.inverse, s32[4]{0:T(128)} %lengths.1, bf16[8192,1024]{1,0:T(8,128)(2,1)} %wq.1, bf16[8192,128]{1,0:T(8,128)(2,1)} %wk.1, bf16[8192,128]{1,0:T(8,128)(2,1)} %wv.1, ...), custom_call_target="tpu_custom_call" | custom-call | tf_op jit(solution)/shard_map/layer/pallas_call | solution.py:762
  121.3 2.1 %copy.13 = bf16[1,3,128,1024]{3,2,1,0:T(8,128)(2,1)} copy(bf16[1,3,128,1024]{3,2,1,0:T(8,128)(2,1)} %bitcast.2) | data formatting | bytes 1572864

commit v5 on v4

--- a/solution.py
+++ b/solution.py
@@ -181,7 +181,7 @@
         after_weights()
 
     units = kvt.shape[0] * raw.shape[0]
-    per_piece = -(-units // (2 * parts * (reach - 1)))
+    per_piece = -(-units // (2 * parts))
 
     def reorder(unit):
         @pl.when(unit < units)
@@ -253,6 +253,10 @@
         remote(xg.at[block, c], block, c, 0, across).wait_recv()
 
     def along(k, carry):
+        @pl.when(k == 2)
+        def _():
+            lax.fori_loop(1, n, send_stored, 0)
+
         def piece(number, carry):
             c, side = lax.div(number, 2), lax.rem(number, 2)
             block = source(k, side, column)
@@ -271,7 +275,6 @@
         return lax.fori_loop(0, 2 * parts, piece, carry)
 
     lax.fori_loop(1, reach, along, 0)
-    lax.fori_loop(1, n, send_stored, 0)
     own = pltpu.make_async_copy(kvt.at[lax.div(me, share)], ctx.at[me], own_sem)
     own.start()
 

time: 124 us -> 124 us (level)
  no operation moved by 1% of the time
where the time goes in v5:
time: 124 us
  Pallas kernels  122 us (98%)
  local copies, waits for them, and re-layouts  2.06 us (2%)
    pallas_call x1, Pallas kernels, layer(): pl.pallas_call(functools.partial(layer_kernel, order, grid, seqs, len(scr...  122 us

profile of v5, /device:TPU:0, one launch (start us, length us, event | category | flops | bytes accessed | tf_op | source)
XLA Modules:
  0.0 124.0 jit_solution(18320378784449267732)
XLA Ops:
  0.0 121.9 %layer.1 = bf16[3,128,1024]{2,1,0:T(8,128)(2,1)} custom-call(bf16[256,1024]{1,0:T(8,128)(2,1)} %tok.1, f32[1,8192]{1,0:T(1,128)} %bitcast.3, f32[1,128]{1,0:T(1,128)} %constant.2.clone.inverse, s32[4]{0:T(128)} %lengths.1, bf16[8192,1024]{1,0:T(8,128)(2,1)} %wq.1, bf16[8192,128]{1,0:T(8,128)(2,1)} %wk.1, bf16[8192,128]{1,0:T(8,128)(2,1)} %wv.1, ...), custom_call_target="tpu_custom_call" | custom-call | tf_op jit(solution)/shard_map/layer/pallas_call | solution.py:765
  121.9 2.1 %copy.13 = bf16[1,3,128,1024]{3,2,1,0:T(8,128)(2,1)} copy(bf16[1,3,128,1024]{3,2,1,0:T(8,128)(2,1)} %bitcast.2) | data formatting | bytes 1572864
